TPU v7x, 128 devices: a whole 4x4x4 slice. The times are simulated.
128 devices in a mesh: row: 8 (over y, x_hi), col: 16 (over z, x_lo, core).
Axes of the slice: x: 4 (x_hi: 2, x_lo: 2; x = x_hi * 2 + x_lo), y: 4, z: 4, core: 2. Of those that a mesh axis runs over, the one named last changes fastest.
Arguments:
- alignment_embedding: bfloat16 [512, 768, 256], P(None, ('row', 'col')), may hold values from -6 to 6
- chosen_sequence_ids: int32 [128], replicated, may hold values from 0 to 511, as said below
- standardizer_scale: float32 [256], replicated, may hold values from 0.1 to 1.9
- standardizer_offset: float32 [256], replicated, may hold values from -3 to 3
- first_factor_matrix: bfloat16 [256, 32], replicated, may hold values from -0.375 to 0.375
- first_factor_shift: float32 [32], replicated, may hold values from -3 to 3
- second_factor_matrix: bfloat16 [256, 32], replicated, may hold values from -0.375 to 0.375
- second_factor_shift: float32 [32], replicated, may hold values from -3 to 3
- final_matrix: bfloat16 [1024, 128], replicated, may hold values from -0.1875 to 0.1875
- twosite_delta_cotangent: bfloat16 [768, 768, 128], P('row', 'col'), may hold values from -6 to 6
Outputs:
- chosen_sequence_slope: bfloat16 [128, 768, 256], P(None, ('row', 'col'))
- first_factor_matrix_slope: float32 [256, 32], replicated
- second_factor_matrix_slope: float32 [256, 32], replicated
- output_weight_gradient: float32 [1024, 128], replicated
Inputs may be any that keep to these rules, and one draw needn't show every extreme that they name: `chosen_sequence_ids`: distinct row indices.
All inputs are finite; a program needn't handle non-finite values.
Results may differ from a plain program's by a relative error of at most 0.02.
Values may be sent and summed in bfloat16 or wider, within the bound.
A program may use at most 192 MiB of HBM per device.

v0:
```python
import jax
import jax.numpy as jnp
from jax import lax
from jax.sharding import PartitionSpec as P

CHOSEN_SEQUENCES = 128


def shards(
    alignment_embedding,
    chosen_sequence_ids,
    standardizer_scale,
    standardizer_offset,
    first_factor_matrix,
    first_factor_shift,
    second_factor_matrix,
    second_factor_shift,
    final_matrix,
    twosite_delta_cotangent,
):
    chosen_alignment_lines = jnp.take(alignment_embedding, chosen_sequence_ids, axis=0)
    element_numbers = chosen_alignment_lines.astype(jnp.float32)
    centered_input = jnp.mean(element_numbers, axis=-1, keepdims=True)
    spread = jnp.mean((element_numbers - centered_input) ** 2, axis=-1, keepdims=True)
    reciprocal_spread = lax.rsqrt(spread + 1e-05)
    whitened_embedding = (element_numbers - centered_input) * reciprocal_spread
    normalized_rows = (whitened_embedding * standardizer_scale + standardizer_offset).astype(
        jnp.bfloat16
    )
    proj_a = (
        jnp.einsum(
            "src,cp->srp", normalized_rows, first_factor_matrix, preferred_element_type=jnp.float32
        )
        + first_factor_shift
    ).astype(jnp.bfloat16)
    proj_b = (
        jnp.einsum(
            "src,cp->srp", normalized_rows, second_factor_matrix, preferred_element_type=jnp.float32
        )
        + second_factor_shift
    ).astype(jnp.bfloat16)
    n_row = lax.axis_size("row")
    n_col = lax.axis_size("col")
    res_dev = proj_a.shape[1]
    sel_rows = proj_a.shape[0]
    feature_width = proj_a.shape[2]
    i_block = res_dev * n_col
    j_block = res_dev * n_row
    col_id = lax.axis_index("col")
    rows_a = lax.all_gather(proj_a, "col", axis=1, tiled=True)
    every_b = lax.all_gather(proj_b, ("row", "col"), axis=1, tiled=True)
    cols_b = lax.dynamic_slice_in_dim(every_b, col_id * j_block, j_block, 1)
    left_flat = rows_a.reshape(sel_rows, i_block * feature_width)
    right_flat = cols_b.reshape(sel_rows, j_block * feature_width)
    outer = lax.dot_general(
        left_flat, right_flat, (((0,), (0,)), ((), ())), preferred_element_type=jnp.float32
    )
    outer = (
        (outer / CHOSEN_SEQUENCES)
        .astype(jnp.bfloat16)
        .reshape(i_block, feature_width, j_block, feature_width)
    )
    final_matrix_slope = jnp.einsum(
        "icje,ijk->cek", outer, twosite_delta_cotangent, preferred_element_type=jnp.float32
    )
    d_outer = jnp.einsum(
        "ijk,fk->ijf", twosite_delta_cotangent, final_matrix, preferred_element_type=jnp.float32
    )
    d_outer = d_outer.astype(jnp.bfloat16).reshape(i_block, j_block, feature_width, feature_width)
    part_a = (
        jnp.einsum("ijce,sje->sic", d_outer, cols_b, preferred_element_type=jnp.float32)
        / CHOSEN_SEQUENCES
    )
    part_b = (
        jnp.einsum("ijce,sic->sje", d_outer, rows_a, preferred_element_type=jnp.float32)
        / CHOSEN_SEQUENCES
    )
    d_a = lax.psum_scatter(part_a.astype(jnp.bfloat16), "col", scatter_dimension=1, tiled=True)
    placed = jnp.zeros((sel_rows, j_block * n_col, feature_width), jnp.float32)
    placed = lax.dynamic_update_slice_in_dim(placed, part_b, col_id * j_block, 1)
    d_b = lax.psum_scatter(placed, ("row", "col"), scatter_dimension=1, tiled=True)
    d_b = d_b.astype(jnp.bfloat16)
    part_w_a = jnp.einsum("src,srp->cp", normalized_rows, d_a, preferred_element_type=jnp.float32)
    part_w_b = jnp.einsum("src,srp->cp", normalized_rows, d_b, preferred_element_type=jnp.float32)
    output_weight_gradient, first_factor_matrix_slope, second_factor_matrix_slope = lax.psum(
        (final_matrix_slope, part_w_a, part_w_b), ("row", "col")
    )
    d_normed = jnp.einsum(
        "srp,cp->src", d_a, first_factor_matrix, preferred_element_type=jnp.float32
    )
    d_normed = d_normed + jnp.einsum(
        "srp,cp->src", d_b, second_factor_matrix, preferred_element_type=jnp.float32
    )
    scaled_by_coefficient = d_normed * standardizer_scale
    chosen_sequence_slope = reciprocal_spread * (
        scaled_by_coefficient
        - jnp.mean(scaled_by_coefficient, axis=-1, keepdims=True)
        - whitened_embedding
        * jnp.mean(scaled_by_coefficient * whitened_embedding, axis=-1, keepdims=True)
    )
    return (
        chosen_sequence_slope.astype(jnp.bfloat16),
        first_factor_matrix_slope,
        second_factor_matrix_slope,
        output_weight_gradient.reshape(feature_width * feature_width, -1),
    )


def solution(mesh):
    return jax.shard_map(
        shards,
        mesh=mesh,
        in_specs=(
            P(None, ("row", "col"), None),
            P(),
            P(),
            P(),
            P(),
            P(),
            P(),
            P(),
            P(),
            P("row", "col", None),
        ),
        out_specs=(P(None, ("row", "col"), None), P(), P(), P()),
        check_vma=False,
    )
```

profile of v0, /device:TPU:1, one launch (start us, length us, event | category | flops | bytes accessed | tf_op | source)
XLA Modules:
  0.0 1246.6 jit_solution(17578363999280212502)
XLA Ops:
  8.7 1.8 gather_fusion
  11.1 1.8 fusion.5
  13.0 7.5 convolution_convert_fusion
  20.5 15.6 %copy.33 = bf16[96,48,1024]{0,2,1:T(8,128)(2,1)} copy(bf16[96,48,1024]{2,1,0:T(8,128)(2,1)} %convolution_convert_fusion) | data formatting | bytes 18874368 | tf_op jit(solution)/shard_map/convert_element_type | solution.py:69
  36.1 27.9 %copy.36 = bf16[96,48,32,32]{1,2,0,3:T(8,128)(2,1)} copy(bf16[96,48,32,32]{0,3,2,1:T(8,128)(2,1)} %bitcast.58) | data formatting | bytes 18874368 | tf_op jit(solution)/shard_map/reshape | solution.py:69
  64.5 27.5 %all_gather.7 = bf16[128,96,32]{0,2,1:T(8,128)(2,1)S(1)} all-gather(bf16[128,6,32]{0,2,1:T(8,128)(2,1)S(1)} %fusion.6), channel_id=1, replica_groups=mesh['row'=8,'col'=16] {'col'}, dimensions={1}, use_global_device_ids=true | all-gather | bytes 835584 | tf_op jit(solution)/shard_map/all_gather | solution.py:50
  92.0 125.9 %all-gather.2.cloned.1.call-done = bf16[128,768,32]{0,2,1:T(8,128)(2,1)} async-done(((bf16[128,6,32]{0,2,1:T(8,128)(2,1)}), bf16[128,768,32]{0,2,1:T(8,128)(2,1)}) %all-gather.2.cloned.1.call-update) | async-done | bytes 6291472 | tf_op jit(solution)/shard_map/all_gather | solution.py:51
  218.9 9.1 fusion
  228.0 1.2 copy.35
  229.2 11.7 fusion.2
  240.9 6.1 broadcast_in_dim.27
  248.4 5.2 multiply_convert_fusion
  253.6 41.2 %reshape.55 = bf16[96,32,48,32]{3,2,1,0:T(8,128)(2,1)} reshape(bf16[3072,1536]{1,0:T(8,128)(2,1)} %multiply_convert_fusion) | data formatting | bytes 18874368 | tf_op jit(solution)/shard_map/reshape | solution.py:61
  294.8 17.1 %fusion.3 = f32[32,32,128,1]{2,1,0,3:T(8,128)} fusion(bf16[96,32,48,32]{3,2,1,0:T(8,128)(2,1)} %reshape.55, bf16[96,48,128]{2,1,0:T(8,128)(2,1)S(1)} %copy-done.2), kind=kOutput, calls=%fused_computation.9 | convolution fusion | flops 1207959552 | bytes 11141120 | tf_op jit(solution)/shard_map/icje,ijk->cek/dot_general | solution.py:63
  312.0 1.8 convolution_bitcast_fusion.2
  314.9 626.5 %reduce-scatter.5.cloned.1.call-done = f32[128,6,32]{0,2,1:T(8,128)} async-done(((f32[128,768,32]{0,2,1:T(8,128)}), f32[128,6,32]{0,2,1:T(8,128)}) %reduce-scatter.5.cloned.1.call-update) | async-done | bytes 98320 | tf_op jit(solution)/shard_map/reduce_scatter | solution.py:81
  941.4 1.7 fusion.33
  943.0 1.9 convolution_bitcast_fusion.1
  945.0 1.9 fusion.17
  946.9 145.5 %all-reduce.4.cloned.1.call-done = f32[1024,128]{1,0:T(8,128)} async-done(((f32[1024,128]{1,0:T(8,128)}), f32[1024,128]{1,0:T(8,128)}) %all-reduce.4.cloned.1.call-update) | async-done | bytes 524304 | tf_op jit(solution)/shard_map/psum | solution.py:85
  1092.4 143.0 %all-reduce.6.cloned.1.call-done = (f32[256,32]{0,1:T(8,128)}, f32[256,32]{0,1:T(8,128)}) async-done(((f32[256,32]{0,1:T(8,128)}, f32[256,32]{0,1:T(8,128)}), (f32[256,32]{0,1:T(8,128)}, f32[256,32]{0,1:T(8,128)})) %all-reduce.6.cloned.1.call-update) | async-done | bytes 65552 | tf_op jit(solution)/shard_map/psum | solution.py:85
  1235.4 1.4 copy.48
  1236.8 1.4 copy.49
  1238.2 1.9 copy.50
  (39 shorter events, 6.2 us)
Async XLA Ops:
  7.2 1.5 copy-start
  7.2 210.7 %all-gather.2.cloned.1.call-start = ((), (), s32[]{:S(2)}) async-start(), calls=%async_computation.2 | async-start | bytes 6340608 | tf_op jit(solution)/shard_map/all_gather | solution.py:51
  8.7 303.3 %copy-start.4 = (pred[128]{0:T(512)(128)(4,1)}, pred[128]{0:T(512)(128)(4,1)S(1)}, u32[]{:S(2)}) copy-start(pred[128]{0:T(512)(128)(4,1)S(1)} %compare_and_fusion) | copy-start | bytes 388
  12.9 299.0 %reduce-scatter.3.cloned.1.call-start = ((), (), s32[]{:S(2)}) async-start(), calls=%async_computation.3 | async-start | bytes 835584 | tf_op jit(solution)/shard_map/reduce_scatter | solution.py:78
  36.1 27.9 %copy-start.3 = (bf16[256,32]{0,1:T(8,128)(2,1)S(1)}, bf16[256,32]{0,1:T(8,128)(2,1)}, u32[]{:S(2)}) copy-start(bf16[256,32]{0,1:T(8,128)(2,1)} %param.14) | copy-start | bytes 49156
  36.1 27.9 %copy-start.5 = (f32[256]{0:T(256)S(1)}, f32[256]{0:T(256)}, u32[]{:S(2)}) copy-start(f32[256]{0:T(256)} %param.12) | copy-start | bytes 3076
  36.1 27.9 %copy-start.6 = (f32[256]{0:T(256)S(1)}, f32[256]{0:T(256)}, u32[]{:S(2)}) copy-start(f32[256]{0:T(256)} %param.13) | copy-start | bytes 3076
  36.1 27.9 %copy-start.7 = (f32[32]{0:T(128)S(1)}, f32[32]{0:T(128)}, u32[]{:S(2)}) copy-start(f32[32]{0:T(128)} %param.15) | copy-start | bytes 388
  229.2 712.2 %reduce-scatter.5.cloned.1.call-start = ((), (), s32[]{:S(2)}) async-start(), calls=%async_computation.4 | async-start | bytes 12681216 | tf_op jit(solution)/shard_map/reduce_scatter | solution.py:81
  248.2 844.3 %all-reduce.4.cloned.1.call-start = ((), (), s32[]{:S(2)}) async-start(), calls=%async_computation.5 | async-start | bytes 1048576 | tf_op jit(solution)/shard_map/psum | solution.py:85
  253.6 41.2 %copy-start.2 = (bf16[96,48,128]{2,1,0:T(8,128)(2,1)S(1)}, bf16[96,48,128]{2,1,0:T(8,128)(2,1)}, u32[]{:S(2)}) copy-start(bf16[96,48,128]{2,1,0:T(8,128)(2,1)} %param.19) | copy-start | bytes 3538948
  294.8 945.3 %copy-start.1 = (bf16[512,6,256]{2,0,1:T(8,128)(2,1)S(1)}, bf16[512,6,256]{2,0,1:T(8,128)(2,1)}, u32[]{:S(2)}) copy-start(bf16[512,6,256]{2,0,1:T(8,128)(2,1)} %param.10) | copy-start | bytes 4718596
  311.9 923.5 %all-reduce.6.cloned.1.call-start = ((), (), s32[]{:S(2)}) async-start(), calls=%async_computation.6 | async-start | bytes 131072 | tf_op jit(solution)/shard_map/psum | solution.py:85
Sparse Core Ops, SparseCore 0:
  13.1 204.7 all-gather.1
  229.3 56.3 reduce-scatter.2
  288.2 653.1 reduce-scatter.4
  946.6 145.8 all-reduce.3
  1098.6 136.7 all-reduce.5
where the time goes:
time: 1250 us
  waiting for transfers between devices  1040 us (83%)
  local copies, waits for them, and re-layouts  101 us (8%)
  matrix products  59.3 us (5%)
  blocking collectives  27.5 us (2%)
  between operations  13.9 us (1%)
    reduce_scatter x1, waiting for transfers between devices, shards(): lax.psum_scatter(placed, ('row', 'col'), scatter_dimension=1, tiled=True)  626 us
    psum x2, waiting for transfers between devices, shards(): lax.psum((final_matrix_slope, part_w_a, part_w_b), ('row', 'col'))  289 us
    all_gather x1, waiting for transfers between devices, shards(): every_b = lax.all_gather(proj_b, ('row', 'col'), axis=1, tiled=True)  126 us
    reshape x1, local copies, waits for them, and re-layouts, shards(): outer = (outer / CHOSEN_SEQUENCES).astype(jnp.bfloat16).reshape(i_block,...  41.2 us
    reshape x1, local copies, waits for them, and re-layouts, shards(): d_outer.astype(jnp.bfloat16)  27.9 us
    all_gather x1, blocking collectives, shards(): rows_a = lax.all_gather(proj_a, 'col', axis=1, tiled=True)  27.5 us
  transfers between devices with their start and end apart: 5, of which 4 were waited for; matrix products, arithmetic and copies ran while one was open for 11% of the time, Pallas kernels for 0%

commit v1 on v0

v1 whole, which is shorter than its diff:
```python
import functools

import jax
import jax.numpy as jnp
from jax import lax
from jax.experimental import pallas as pl
from jax.experimental.pallas import tpu as pltpu
from jax.sharding import PartitionSpec as P

CHOSEN_SEQUENCES = 128
SLOT = 8

BF = jnp.bfloat16
F32 = jnp.float32
NN = (((1,), (0,)), ((), ()))
NT = (((1,), (1,)), ((), ()))


def dot(left, right, dims=NN):
    return lax.dot_general(left, right, dims, preferred_element_type=F32)


def kernel(
    emb_ref, ids_ref, scale_ref, offset_ref, w_a_ref, w_b_ref, shift_ref, final_ref, dz_ref,
    slope_ref, grad_a_ref, grad_b_ref, grad_w_ref,
    xhat_ref, inv_ref, normed_ref, dzf_ref, dzb_ref, d_ref, o_ref,
    abuf, bsend, bbuf, atf_ref, at_ref, bt_ref, daf_ref, sa, ra, sb, rb,
    sw, rw, sw2, rw2, fw, wacc_ref, sp, rp, sp2, rp2, fp,
    ssem_a, rsem_a, ssem_b, rsem_b, ssem_ra, rsem_ra, ssem_rb, rsem_rb,
    ssem_w, rsem_w, ssem_w2, rsem_w2, ssem_w3, rsem_w3,
    ssem_p, rsem_p, ssem_p2, rsem_p2, ssem_p3, rsem_p3,
):
    n_row, n_col = bbuf.shape[0], abuf.shape[0]
    n_res, n_sel, width = normed_ref.shape
    rank = w_a_ref.shape[0]
    n_j = n_row * n_res
    lanes = n_col * SLOT
    chunk = n_res * rank
    row, col = lax.axis_index("row"), lax.axis_index("col")
    me = row * n_col + col
    b_col, b_slot = me // n_row, me % n_row

    def copy(src, dst, send_sem, recv_sem, device):
        return pltpu.make_async_remote_copy(
            src_ref=src, dst_ref=dst, send_sem=send_sem, recv_sem=recv_sem,
            device_id=device, device_id_type=pl.DeviceIdType.MESH,
        )

    def each(count, body):
        lax.fori_loop(0, count, lambda i, _: (body(i), None)[1], None)

    def col_peer(t):
        return lax.rem(col + t, n_col)

    def row_peer(t):
        return lax.rem(row + t, n_row)

    def source(k):
        block = n_row * col + k
        return block // n_col, block % n_col

    barrier = pltpu.get_barrier_semaphore()

    def greet(device):
        pl.semaphore_signal(barrier, inc=1, device_id=device, device_id_type=pl.DeviceIdType.MESH)

    each(n_col - 1, lambda t: greet((row, col_peer(t + 1))))
    each(n_row - 1, lambda t: greet((row_peer(t + 1), col)))

    def greet_b(k):
        src = source(k)

        @pl.when(n_row * col + k != me)
        def _():
            greet(src)

        @pl.when(jnp.logical_or(k != row, b_col != col))
        def _():
            greet((k, b_col))

    each(n_row, greet_b)

    picks = (
        lax.broadcasted_iota(jnp.int32, (n_sel, emb_ref.shape[1]), 1) == ids_ref[...]
    ).astype(F32).astype(BF)
    w_both = jnp.concatenate([w_a_ref[...], w_b_ref[...]], axis=0)
    for r in range(n_res):
        x = dot(picks, emb_ref[r])
        centred = x - jnp.mean(x, axis=-1, keepdims=True)
        inverse = lax.rsqrt(jnp.mean(centred * centred, axis=-1, keepdims=True) + 1e-05)
        xhat = centred * inverse
        xhat_ref[r] = xhat
        inv_ref[r] = inverse
        normed = (xhat * scale_ref[...] + offset_ref[...]).astype(BF)
        normed_ref[r] = normed
        proj = (dot(w_both, normed, NT) + shift_ref[...]).astype(BF)
        abuf[col, r * rank : (r + 1) * rank, :] = proj[:rank]
        bsend[r * rank : (r + 1) * rank, :] = proj[rank:]

    self_b = jnp.where(b_col == col, 1, 0)
    pl.semaphore_wait(barrier, (n_col - 1) + (n_row - 1) + 2 * (n_row - self_b))

    def b_copy(k):
        return copy(bsend, bbuf.at[b_slot], ssem_b.at[k], rsem_b.at[b_slot], (k, b_col))

    def send_b(t):
        k = row_peer(t)

        @pl.when(jnp.logical_or(k != row, b_col != col))
        def _():
            b_copy(k).start()

    @pl.when(b_col == col)
    def _():
        bbuf[b_slot] = bsend[...]

    each(n_row, send_b)

    def a_copy(t, peer):
        return copy(abuf.at[col], abuf.at[col], ssem_a.at[t], rsem_a.at[col], (row, peer))

    each(n_col - 1, lambda t: a_copy(t, col_peer(t + 1)).start())

    n_i, j_width, k_width = dz_ref.shape
    dzf_ref[pl.ds(0, n_i * j_width), :] = dz_ref[...].astype(F32).reshape(n_i * j_width, k_width)
    dzf_ref[pl.ds(n_i * j_width, 2 * j_width), :] = jnp.zeros((2 * j_width, k_width), F32)
    atf_ref[...] = jnp.zeros(atf_ref.shape, F32)

    def spread(j):
        rows = [
            dzf_ref[pl.ds(n_res * q * j_width + j, SLOT, stride=j_width), :] for q in range(n_col)
        ]
        dzb_ref[j] = jnp.concatenate(rows, axis=0).astype(BF)

    each(n_j, spread)

    def d_step(step):
        pair = dzb_ref[pl.ds(2 * step, 2)].reshape(2 * lanes, k_width)
        d = dot(final_ref[...], pair, NT).astype(BF)
        for q in range(2):
            at = pl.ds(pl.multiple_of((2 * step + q) * rank, rank), rank)
            d_ref[:, at, :] = d[:, q * lanes : (q + 1) * lanes].reshape(rank, rank, lanes)

    each(n_j // 2, d_step)

    def wait_b(k):
        @pl.when(n_row * col + k != me)
        def _():
            copy(bsend, bbuf.at[k], ssem_b.at[k], rsem_b.at[k], source(k)).wait_recv()

    each(n_row, wait_b)
    right_t = bbuf[...].reshape(n_j * rank, n_sel)
    bt_ref[...] = right_t.T

    def part_a_step(step):
        d = jnp.concatenate([d_ref[2 * step], d_ref[2 * step + 1]], axis=1)
        part = dot(bt_ref[...], d) * (1.0 / CHOSEN_SEQUENCES)
        for q in range(2):
            at = pl.ds(pl.multiple_of((2 * step + q) * lanes, lanes), lanes)
            daf_ref[at, :] = part[:, q * lanes : (q + 1) * lanes].T

    each(rank // 2, part_a_step)

    def ra_copy(t, peer):
        return copy(sa.at[peer], ra.at[col], ssem_ra.at[t], rsem_ra.at[col], (row, peer))

    def a_chunk(q):
        return [
            daf_ref[pl.ds(q * SLOT + r, rank, stride=lanes), :].astype(BF) for r in range(n_res)
        ]

    def send_part_a(t):
        peer = col_peer(t + 1)
        for r, piece in enumerate(a_chunk(peer)):
            sa[peer, r * rank : (r + 1) * rank, :] = piece
        ra_copy(t, peer).start()

    each(n_col - 1, send_part_a)
    for r, piece in enumerate(a_chunk(col)):
        ra[col, r * rank : (r + 1) * rank, :] = piece

    def take_a(q):
        for r in range(n_res):
            atf_ref[pl.ds(q * SLOT + r, rank, stride=lanes), :] = abuf[
                q, r * rank : (r + 1) * rank, :
            ].astype(F32)

    take_a(col)

    def wait_a(t):
        q = col_peer(n_col - 1 - t)
        copy(abuf.at[q], abuf.at[q], ssem_a.at[t], rsem_a.at[q], (row, q)).wait_recv()
        take_a(q)

    each(n_col - 1, wait_a)

    def cast_a(c):
        at = pl.ds(pl.multiple_of(c * 4 * lanes, 4 * lanes), 4 * lanes)
        at_ref[at, :] = atf_ref[at, :].astype(BF)

    each(rank // 4, cast_a)

    def rb_copy(k, device):
        return copy(sb.at[k], rb.at[row], ssem_rb.at[k], rsem_rb.at[row], device)

    def part_b_step(k):
        at = pl.ds(pl.multiple_of(k * chunk, chunk), chunk)
        total = jnp.zeros((chunk, n_sel), F32)
        for c in range(0, rank, 2):
            d = jnp.concatenate([d_ref[c, at, :], d_ref[c + 1, at, :]], axis=1)
            total += dot(d, at_ref[c * lanes : (c + 2) * lanes, :])
        total = (total * (1.0 / CHOSEN_SEQUENCES)).astype(BF)
        sb[k] = total

        @pl.when(n_row * col + k == me)
        def _():
            rb[row] = total

        @pl.when(n_row * col + k != me)
        def _():
            rb_copy(k, source(k)).start()

    each(n_row, part_b_step)

    def o_step(step):
        at = pl.ds(pl.multiple_of(2 * step * lanes, 2 * lanes), 2 * lanes)
        o = dot(bbuf[...].reshape(n_j * rank, n_sel), at_ref[at, :], NT).astype(BF)
        o_ref[2 * step] = o[:, :lanes]
        o_ref[2 * step + 1] = o[:, lanes:]

    each(rank // 2, o_step)

    wacc_ref[...] = jnp.zeros(wacc_ref.shape, F32)

    def w_step(step):
        pieces = []
        for q in range(4):
            at = pl.ds(pl.multiple_of((4 * step + q) * rank, rank), rank)
            pieces.append(o_ref[:, at, :].reshape(rank * rank, lanes))
        z = dzb_ref[pl.ds(4 * step, 4)].reshape(4 * lanes, k_width)
        wacc_ref[...] += dot(jnp.concatenate(pieces, axis=1), z)

    each(n_j // 4, w_step)
    sw[...] = (wacc_ref[...] * (1.0 / CHOSEN_SEQUENCES)).astype(BF).reshape(sw.shape)

    def w_copy(t, peer):
        return copy(sw.at[peer], rw.at[col], ssem_w.at[t], rsem_w.at[col], (row, peer))

    each(n_col - 1, lambda t: w_copy(t, col_peer(t + 1)).start())
    rw[col] = sw[col]

    def wait_ra(t):
        q = col_peer(n_col - 1 - t)
        copy(sa.at[q], ra.at[q], ssem_ra.at[t], rsem_ra.at[q], (row, q)).wait_recv()

    each(n_col - 1, wait_ra)

    def wait_rb(k):
        @pl.when(jnp.logical_or(k != row, b_col != col))
        def _():
            copy(sb.at[k], rb.at[k], ssem_rb.at[k], rsem_rb.at[k], (k, b_col)).wait_recv()

    each(n_row, wait_rb)

    d_a = jnp.sum(ra[...].astype(F32), axis=0).astype(BF)
    d_b = jnp.sum(rb[...].astype(F32), axis=0).astype(BF)
    d_both = [
        jnp.concatenate(
            [d_a[r * rank : (r + 1) * rank], d_b[r * rank : (r + 1) * rank]], axis=0
        )
        for r in range(n_res)
    ]
    part_p = jnp.zeros((2 * rank, width), F32)
    for r in range(n_res):
        part_p += dot(d_both[r], normed_ref[r])
    half = width // 2
    sp[...] = jnp.concatenate([part_p[:, :half], part_p[:, half:]], axis=0).reshape(sp.shape)

    def p_copy(t, peer):
        return copy(sp.at[peer], rp.at[col], ssem_p.at[t], rsem_p.at[col], (row, peer))

    each(n_col - 1, lambda t: p_copy(t, col_peer(t + 1)).start())
    rp[col] = sp[col]

    def wait_w(t):
        q = col_peer(n_col - 1 - t)
        copy(sw.at[q], rw.at[q], ssem_w.at[t], rsem_w.at[q], (row, q)).wait_recv()

    each(n_col - 1, wait_w)
    sw2[...] = jnp.sum(rw[...].astype(F32), axis=0).astype(BF)
    rw2[row] = sw2[...]

    def w2_copy(t, peer):
        return copy(sw2, rw2.at[row], ssem_w2.at[t], rsem_w2.at[row], (peer, col))

    each(n_row - 1, lambda t: w2_copy(t, row_peer(t + 1)).start())

    def layer_norm_back(r):
        g = lax.dot_general(
            d_both[r], w_both, (((0,), (0,)), ((), ())), preferred_element_type=F32
        )
        g = g * scale_ref[...]
        xhat = xhat_ref[r]
        slope = inv_ref[r] * (
            g
            - jnp.mean(g, axis=-1, keepdims=True)
            - xhat * jnp.mean(g * xhat, axis=-1, keepdims=True)
        )
        slope_ref[r] = slope.astype(BF)

    for r in range(n_res // 2):
        layer_norm_back(r)

    def wait_p(t):
        q = col_peer(n_col - 1 - t)
        copy(sp.at[q], rp.at[q], ssem_p.at[t], rsem_p.at[q], (row, q)).wait_recv()

    each(n_col - 1, wait_p)
    sp2[...] = jnp.sum(rp[...], axis=0)
    rp2[row] = sp2[...]

    def p2_copy(t, peer):
        return copy(sp2, rp2.at[row], ssem_p2.at[t], rsem_p2.at[row], (peer, col))

    each(n_row - 1, lambda t: p2_copy(t, row_peer(t + 1)).start())

    def wait_w2(t):
        q = row_peer(n_row - 1 - t)
        copy(sw2, rw2.at[q], ssem_w2.at[t], rsem_w2.at[q], (q, col)).wait_recv()

    each(n_row - 1, wait_w2)
    fw[col] = jnp.sum(rw2[...].astype(F32), axis=0).astype(BF)

    def w3_copy(t, peer):
        return copy(fw.at[col], fw.at[col], ssem_w3.at[t], rsem_w3.at[col], (row, peer))

    each(n_col - 1, lambda t: w3_copy(t, col_peer(t + 1)).start())

    for r in range(n_res // 2, n_res):
        layer_norm_back(r)

    def wait_p2(t):
        q = row_peer(n_row - 1 - t)
        copy(sp2, rp2.at[q], ssem_p2.at[t], rsem_p2.at[q], (q, col)).wait_recv()

    each(n_row - 1, wait_p2)
    fp[col] = jnp.sum(rp2[...], axis=0)

    def p3_copy(t, peer):
        return copy(fp.at[col], fp.at[col], ssem_p3.at[t], rsem_p3.at[col], (row, peer))

    each(n_col - 1, lambda t: p3_copy(t, col_peer(t + 1)).start())

    def wait_w3(t):
        q = col_peer(n_col - 1 - t)
        copy(fw.at[q], fw.at[q], ssem_w3.at[t], rsem_w3.at[q], (row, q)).wait_recv()

    each(n_col - 1, wait_w3)
    grad_w_ref[...] = fw[...].astype(F32).reshape(grad_w_ref.shape)

    def wait_p3(t):
        q = col_peer(n_col - 1 - t)
        copy(fp.at[q], fp.at[q], ssem_p3.at[t], rsem_p3.at[q], (row, q)).wait_recv()

    each(n_col - 1, wait_p3)
    both = fp[...].reshape(4 * rank, half)
    grad_a_ref[...] = jnp.concatenate([both[:rank], both[2 * rank : 3 * rank]], axis=1)
    grad_b_ref[...] = jnp.concatenate([both[rank : 2 * rank], both[3 * rank :]], axis=1)

    def sent_b(k):
        @pl.when(jnp.logical_or(k != row, b_col != col))
        def _():
            b_copy(k).wait_send()

        @pl.when(n_row * col + k != me)
        def _():
            rb_copy(k, source(k)).wait_send()

    each(n_row, sent_b)

    def sent_col(t):
        peer = col_peer(t + 1)
        for made in (a_copy, ra_copy, w_copy, w3_copy, p_copy, p3_copy):
            made(t, peer).wait_send()

    each(n_col - 1, sent_col)

    def sent_row(t):
        peer = row_peer(t + 1)
        for made in (w2_copy, p2_copy):
            made(t, peer).wait_send()

    each(n_row - 1, sent_row)


def shards(
    n_row,
    n_col,
    alignment_embedding,
    chosen_sequence_ids,
    standardizer_scale,
    standardizer_offset,
    first_factor_matrix,
    first_factor_shift,
    second_factor_matrix,
    second_factor_shift,
    final_matrix,
    twosite_delta_cotangent,
):
    width, rank = first_factor_matrix.shape
    n_sel = chosen_sequence_ids.shape[0]
    n_res = alignment_embedding.shape[1]
    n_i, n_j, k_width = twosite_delta_cotangent.shape
    lanes = n_col * SLOT
    chunk = n_res * rank
    w_rows = rank * rank // n_col
    p_rows = 4 * rank // n_col
    dma = lambda n: pltpu.SemaphoreType.DMA((n,))
    vmem = pltpu.VMEM
    scratch = [
        vmem((n_res, n_sel, width), F32),
        vmem((n_res, n_sel, 1), F32),
        vmem((n_res, n_sel, width), BF),
        vmem(((n_i + 2) * n_j, k_width), F32),
        vmem((n_j, lanes, k_width), BF),
        vmem((rank, n_j * rank, lanes), BF),
        vmem((rank, n_j * rank, lanes), BF),
        vmem((n_col, chunk, n_sel), BF),
        vmem((chunk, n_sel), BF),
        vmem((n_row, chunk, n_sel), BF),
        vmem((rank * lanes, n_sel), F32),
        vmem((rank * lanes, n_sel), BF),
        vmem((n_sel, n_j * rank), BF),
        vmem((rank * lanes, n_sel), F32),
        vmem((n_col, chunk, n_sel), BF),
        vmem((n_col, chunk, n_sel), BF),
        vmem((n_row, chunk, n_sel), BF),
        vmem((n_row, chunk, n_sel), BF),
        vmem((n_col, w_rows, k_width), BF),
        vmem((n_col, w_rows, k_width), BF),
        vmem((w_rows, k_width), BF),
        vmem((n_row, w_rows, k_width), BF),
        vmem((n_col, w_rows, k_width), BF),
        vmem((rank * rank, k_width), F32),
        vmem((n_col, p_rows, width // 2), F32),
        vmem((n_col, p_rows, width // 2), F32),
        vmem((p_rows, width // 2), F32),
        vmem((n_row, p_rows, width // 2), F32),
        vmem((n_col, p_rows, width // 2), F32),
        *[dma(n) for n in (n_col, n_col, n_row, n_row, n_col, n_col, n_row, n_row)],
        *[dma(n) for n in (n_col, n_col, n_row, n_row, n_col, n_col)],
        *[dma(n) for n in (n_col, n_col, n_row, n_row, n_col, n_col)],
    ]
    whole = pl.BlockSpec(memory_space=pltpu.VMEM)
    shift = jnp.concatenate([first_factor_shift, second_factor_shift]).reshape(2 * rank, 1)
    slope, grad_a, grad_b, grad_w = pl.pallas_call(
        kernel,
        out_shape=(
            jax.ShapeDtypeStruct((n_res, n_sel, width), BF),
            jax.ShapeDtypeStruct((rank, width), F32),
            jax.ShapeDtypeStruct((rank, width), F32),
            jax.ShapeDtypeStruct((rank * rank, k_width), F32),
        ),
        in_specs=[whole] * 9,
        out_specs=(whole,) * 4,
        scratch_shapes=scratch,
        compiler_params=pltpu.CompilerParams(
            collective_id=0, has_side_effects=True, vmem_limit_bytes=60 * 1024 * 1024
        ),
    )(
        alignment_embedding.transpose(1, 0, 2),
        chosen_sequence_ids.reshape(n_sel, 1),
        standardizer_scale.reshape(1, width),
        standardizer_offset.reshape(1, width),
        first_factor_matrix.T,
        second_factor_matrix.T,
        shift,
        final_matrix,
        twosite_delta_cotangent,
    )
    return slope.transpose(1, 0, 2), grad_a.T, grad_b.T, grad_w


def solution(mesh):
    return jax.shard_map(
        functools.partial(shards, mesh.shape["row"], mesh.shape["col"]),
        mesh=mesh,
        in_specs=(
            P(None, ("row", "col"), None),
            P(),
            P(),
            P(),
            P(),
            P(),
            P(),
            P(),
            P(),
            P("row", "col", None),
        ),
        out_specs=(P(None, ("row", "col"), None), P(), P(), P()),
        check_vma=False,
    )
```

time: 1250 us -> 83.2 us (0.07)
  waiting for transfers between devices: 1040 us -> 0 us
  local copies, waits for them, and re-layouts: 101 us -> 8.48 us
  Pallas kernels: 0 us -> 72.9 us
  matrix products: 59.3 us -> 0 us
  blocking collectives: 27.5 us -> 0 us
  between operations: 13.9 us -> 0.64 us
    reduce_scatter x2 -> x0, waiting for transfers between devices: 626 us -> none  [the longest x1 626 us: shards(): lax.psum_scatter(placed, ('row', 'col'), scatter_dimension=1, tiled=True)]
    psum x2 -> x0, waiting for transfers between devices: 289 us -> none  [shards(): lax.psum((final_matrix_slope, part_w_a, part_w_b), ('row', 'col'))]
    all_gather x1 -> x0, waiting for transfers between devices: 126 us -> none  [shards(): every_b = lax.all_gather(proj_b, ('row', 'col'), axis=1, tiled=True)]
    pallas_call x0 -> x1, Pallas kernels: none -> 72.9 us  [shards(): pl.pallas_call(kernel, out_shape=(jax.ShapeDtypeStruct((n_res, n_sel, wid...]
    reshape x2, local copies, waits for them, and re-layouts: 69.1 us -> 2.1 us  [the longest x1 1.39 us: shards(): chosen_sequence_ids.reshape(n_sel, 1)]
    dot_general x11 -> x0, matrix products: 59.3 us -> none  [the longest x1 17.1 us: shards(): jnp.einsum('icje,ijk->cek', outer, twosite_delta_cotangent, preferred_ele...]
    all_gather x1 -> x0, blocking collectives: 27.5 us -> none  [shards(): rows_a = lax.all_gather(proj_a, 'col', axis=1, tiled=True)]
    convert_element_type x2 -> x0, local copies, waits for them, and re-layouts: 16.8 us -> none  [the longest x1 15.6 us: shards(): d_outer.astype(jnp.bfloat16)]
  transfers between devices with their start and end apart: 5 -> 0, of which waited for: 4 -> 0; matrix products, arithmetic and copies ran while one was open for 11% -> 0% of each run, Pallas kernels for 0% -> 0%
where the time goes in v1:
time: 83.2 us; the launch traced here: 82.8 us
  Pallas kernels  72.9 us (88%)
  local copies, waits for them, and re-layouts  8.48 us (10%)
    pallas_call x1, Pallas kernels, shards(): pl.pallas_call(kernel, out_shape=(jax.ShapeDtypeStruct((n_res, n_sel, wid...  72.9 us
    unnamed x4, local copies, waits for them, and re-layouts  6.38 us

profile of v1, /device:TPU:1, one launch (start us, length us, event | category | flops | bytes accessed | tf_op | source)
XLA Modules:
  0.0 82.8 jit_solution(12798414881325290363)
XLA Ops:
  0.6 0.7 maximum_bitcast_fusion
  1.4 0.7 copy.15.shift_ref
  2.1 1.4 %copy.14.ids_ref = s32[128,1]{1,0:T(8,128)} copy(s32[128,1]{0,1:T(1,128)} %bitcast.19) | data formatting | bytes 1024 | tf_op jit(solution)/shard_map/reshape | solution.py:472
  3.5 72.9 %shard_map.129 = (bf16[6,128,256]{2,1,0:T(8,128)(2,1)}, f32[32,256]{1,0:T(8,128)}, f32[32,256]{1,0:T(8,128)}, f32[1024,128]{1,0:T(8,128)}) custom-call(bf16[6,512,256]{2,1,0:T(8,128)(2,1)} %bitcast.11, s32[128,1]{1,0:T(8,128)} %copy.14.ids_ref, f32[1,256]{1,0:T(1,128)} %bitcast.17, f32[1,256]{1,0:T(1,128)} %bitcast.18, bf16[32,256]{1,0:T(8,128)(2,1)} %bitcast.15, ...), custom_call_target="tpu_custom_call" | custom-call | tf_op jit(solution)/shard_map/pallas_call | solution.py:456
  76.4 1.8 %copy.20 = bf16[128,6,256]{2,0,1:T(8,128)(2,1)} copy(bf16[128,6,256]{2,0,1:T(8,128)(2,1)} %bitcast.12) | data formatting | bytes 786432
  78.2 1.4 %copy.21 = f32[256,32]{0,1:T(8,128)} copy(f32[256,32]{0,1:T(8,128)} %bitcast.14) | data formatting | bytes 65536
  79.6 1.4 %copy.22 = f32[256,32]{0,1:T(8,128)} copy(f32[256,32]{0,1:T(8,128)} %bitcast.13) | data formatting | bytes 65536
  80.9 1.9 %copy.23 = f32[1024,128]{1,0:T(8,128)} copy(f32[1024,128]{1,0:T(8,128)} %get-tuple-element.19) | data formatting | bytes 1048576

commit v2 on v1

v2 whole, which is shorter than its diff:
```python
import functools

import jax
import jax.numpy as jnp
from jax import lax
from jax.experimental import pallas as pl
from jax.experimental.pallas import tpu as pltpu
from jax.sharding import PartitionSpec as P

CHOSEN_SEQUENCES = 128
SLOT = 8

BF = jnp.bfloat16
F32 = jnp.float32
NN = (((1,), (0,)), ((), ()))
NT = (((1,), (1,)), ((), ()))


def dot(left, right, dims=NN):
    return lax.dot_general(left, right, dims, preferred_element_type=F32)


def kernel(
    emb_ref, ids_ref, scale_ref, offset_ref, w_a_ref, w_b_ref, shift_ref, final_ref, dz_ref,
    slope_ref, sums_ref,
    xhat_ref, inv_ref, normed_ref, dzf_ref, dzb_ref, d_ref, o_ref,
    abuf, bsend, bbuf, atf_ref, at_ref, bt_ref, daf_ref, sa, ra0, sa1, ra1, sb, rb, wacc_ref,
    st0, rt0, st1, rt1, st2, rt2,
    ssem_a, rsem_a, ssem_a2, rsem_a2, ssem_b, rsem_b, ssem_ra, rsem_ra, ssem_rb, rsem_rb,
    ssem_t1, rsem_t1, ssem_t2, rsem_t2, ssem_t3, rsem_t3, sib_sems,
):
    n_row, n_col = bbuf.shape[0], abuf.shape[0]
    n_chip = n_col // 2
    n_res, n_sel, width = normed_ref.shape
    rank = w_a_ref.shape[0]
    n_j = n_row * n_res
    lanes = n_col * SLOT
    chunk = n_res * rank
    row, col = lax.axis_index("row"), lax.axis_index("col")
    me = row * n_col + col
    b_col, b_slot = me // n_row, me % n_row
    chip, core = col // 2, col % 2
    other = 1 - core
    sibling = (row, col + 1 - 2 * core)

    def copy(src, dst, send_sem, recv_sem, device):
        return pltpu.make_async_remote_copy(
            src_ref=src, dst_ref=dst, send_sem=send_sem, recv_sem=recv_sem,
            device_id=device, device_id_type=pl.DeviceIdType.MESH,
        )

    def each(count, body):
        lax.fori_loop(0, count, lambda i, _: (body(i), None)[1], None)

    def chip_peer(t):
        return lax.rem(chip + t, n_chip)

    def at_chip(q):
        return (row, 2 * q + core)

    def row_peer(t):
        return lax.rem(row + t, n_row)

    def source(k):
        block = n_row * col + k
        return block // n_col, block % n_col

    barrier = pltpu.get_barrier_semaphore()

    def greet(device):
        pl.semaphore_signal(barrier, inc=1, device_id=device, device_id_type=pl.DeviceIdType.MESH)

    greet(sibling)
    each(n_chip - 1, lambda t: greet(at_chip(chip_peer(t + 1))))
    each(n_row - 1, lambda t: greet((row_peer(t + 1), col)))

    def greet_b(k):
        src = source(k)

        @pl.when(n_row * col + k != me)
        def _():
            greet(src)

        @pl.when(jnp.logical_or(k != row, b_col != col))
        def _():
            greet((k, b_col))

    each(n_row, greet_b)

    n_all = emb_ref.shape[1]
    ids = jnp.broadcast_to(ids_ref[...], (n_sel, n_sel)).T
    ids = jnp.concatenate([ids] * (n_all // n_sel), axis=1)
    picks = (lax.broadcasted_iota(jnp.int32, (n_sel, n_all), 1) == ids).astype(F32).astype(BF)
    w_both = jnp.concatenate([w_a_ref[...], w_b_ref[...]], axis=0)
    for r in range(n_res):
        x = dot(picks, emb_ref[r])
        centred = x - jnp.mean(x, axis=-1, keepdims=True)
        inverse = lax.rsqrt(jnp.mean(centred * centred, axis=-1, keepdims=True) + 1e-05)
        xhat = centred * inverse
        xhat_ref[r] = xhat
        inv_ref[r] = inverse
        normed = (xhat * scale_ref[...] + offset_ref[...]).astype(BF)
        normed_ref[r] = normed
        proj = (dot(w_both, normed, NT) + shift_ref[...]).astype(BF)
        abuf[col, r * rank : (r + 1) * rank, :] = proj[:rank]
        bsend[r * rank : (r + 1) * rank, :] = proj[rank:]

    self_b = jnp.where(b_col == col, 1, 0)
    pl.semaphore_wait(barrier, n_chip + (n_row - 1) + 2 * (n_row - self_b))

    def b_copy(k):
        return copy(bsend, bbuf.at[b_slot], ssem_b.at[k], rsem_b.at[b_slot], (k, b_col))

    def send_b(t):
        k = row_peer(t)

        @pl.when(jnp.logical_or(k != row, b_col != col))
        def _():
            b_copy(k).start()

    @pl.when(b_col == col)
    def _():
        bbuf[b_slot] = bsend[...]

    each(n_row, send_b)

    def a_copy(t, q):
        return copy(abuf.at[col], abuf.at[col], ssem_a.at[t], rsem_a.at[chip], at_chip(q))

    def a_forward(q):
        block = abuf.at[2 * q + core]
        return copy(block, block, ssem_a2.at[q], rsem_a2.at[q], sibling)

    each(n_chip - 1, lambda t: a_copy(t, chip_peer(t + 1)).start())
    a_forward(chip).start()

    n_i, j_width, k_width = dz_ref.shape
    dzf_ref[pl.ds(0, n_i * j_width), :] = dz_ref[...].astype(F32).reshape(n_i * j_width, k_width)
    dzf_ref[pl.ds(n_i * j_width, 2 * j_width), :] = jnp.zeros((2 * j_width, k_width), F32)
    atf_ref[...] = jnp.zeros(atf_ref.shape, F32)

    def spread(j):
        rows = [
            dzf_ref[pl.ds(n_res * q * j_width + j, SLOT, stride=j_width), :] for q in range(n_col)
        ]
        dzb_ref[j] = jnp.concatenate(rows, axis=0).astype(BF)

    each(n_j, spread)

    def d_step(step):
        pair = dzb_ref[pl.ds(2 * step, 2)].reshape(2 * lanes, k_width)
        d = dot(final_ref[...], pair, NT).astype(BF)
        for q in range(2):
            at = pl.ds(pl.multiple_of((2 * step + q) * rank, rank), rank)
            d_ref[:, at, :] = d[:, q * lanes : (q + 1) * lanes].reshape(rank, rank, lanes)

    each(n_j // 2, d_step)

    def pass_a(t):
        q = chip_peer(n_chip - 1 - t)
        block = abuf.at[2 * q + core]
        copy(block, block, ssem_a.at[t], rsem_a.at[q], at_chip(q)).wait_recv()
        a_forward(q).start()

    each(n_chip - 1, pass_a)

    def wait_b(k):
        @pl.when(n_row * col + k != me)
        def _():
            copy(bsend, bbuf.at[k], ssem_b.at[k], rsem_b.at[k], source(k)).wait_recv()

    each(n_row, wait_b)
    right_t = bbuf[...].reshape(n_j * rank, n_sel)
    bt_ref[...] = right_t.T

    def part_a_step(step):
        d = jnp.concatenate([d_ref[2 * step], d_ref[2 * step + 1]], axis=1)
        part = dot(bt_ref[...], d) * (1.0 / CHOSEN_SEQUENCES)
        for q in range(2):
            at = pl.ds(pl.multiple_of((2 * step + q) * lanes, lanes), lanes)
            daf_ref[at, :] = part[:, q * lanes : (q + 1) * lanes].T

    each(rank // 2, part_a_step)

    def pack_a(q):
        for k in range(2):
            for r in range(n_res):
                sa[k, q, r * rank : (r + 1) * rank, :] = daf_ref[
                    pl.ds((2 * q + k) * SLOT + r, rank, stride=lanes), :
                ].astype(BF)

    each(n_chip, pack_a)

    def sib_copy(i, src, dst):
        return copy(src, dst, sib_sems.at[i], sib_sems.at[i + 1], sibling)

    ra_sib = sib_copy(0, sa.at[other], ra0)
    ra_sib.start()

    def take_a(q):
        for r in range(n_res):
            atf_ref[pl.ds(q * SLOT + r, rank, stride=lanes), :] = abuf[
                q, r * rank : (r + 1) * rank, :
            ].astype(F32)

    def wait_a(q):
        block = abuf.at[2 * q + other]
        copy(block, block, ssem_a2.at[q], rsem_a2.at[q], sibling).wait_recv()
        take_a(2 * q)
        take_a(2 * q + 1)

    each(n_chip, wait_a)

    def cast_a(c):
        at = pl.ds(pl.multiple_of(c * 4 * lanes, 4 * lanes), 4 * lanes)
        at_ref[at, :] = atf_ref[at, :].astype(BF)

    each(rank // 4, cast_a)

    def ra_copy(t, q):
        return copy(sa1.at[q], ra1.at[chip], ssem_ra.at[t], rsem_ra.at[chip], at_chip(q))

    ra_sib.wait_recv()

    def send_part_a(t):
        q = chip_peer(t + 1)
        sa1[q] = (sa[core, q].astype(F32) + ra0[q].astype(F32)).astype(BF)
        ra_copy(t, q).start()

    each(n_chip - 1, send_part_a)
    ra1[chip] = (sa[core, chip].astype(F32) + ra0[chip].astype(F32)).astype(BF)

    def rb_copy(k, device):
        return copy(sb.at[k], rb.at[row], ssem_rb.at[k], rsem_rb.at[row], device)

    def part_b_step(k):
        at = pl.ds(pl.multiple_of(k * chunk, chunk), chunk)
        total = jnp.zeros((chunk, n_sel), F32)
        for c in range(0, rank, 2):
            d = jnp.concatenate([d_ref[c, at, :], d_ref[c + 1, at, :]], axis=1)
            total += dot(d, at_ref[c * lanes : (c + 2) * lanes, :])
        total = (total * (1.0 / CHOSEN_SEQUENCES)).astype(BF)
        sb[k] = total

        @pl.when(n_row * col + k == me)
        def _():
            rb[row] = total

        @pl.when(n_row * col + k != me)
        def _():
            rb_copy(k, source(k)).start()

    each(n_row, part_b_step)

    def o_step(step):
        at = pl.ds(pl.multiple_of(2 * step * lanes, 2 * lanes), 2 * lanes)
        o = dot(bbuf[...].reshape(n_j * rank, n_sel), at_ref[at, :], NT).astype(BF)
        o_ref[2 * step] = o[:, :lanes]
        o_ref[2 * step + 1] = o[:, lanes:]

    each(rank // 2, o_step)

    wacc_ref[...] = jnp.zeros(wacc_ref.shape, F32)

    def w_step(step):
        pieces = []
        for q in range(4):
            at = pl.ds(pl.multiple_of((4 * step + q) * rank, rank), rank)
            pieces.append(o_ref[:, at, :].reshape(rank * rank, lanes))
        z = dzb_ref[pl.ds(4 * step, 4)].reshape(4 * lanes, k_width)
        wacc_ref[...] += dot(jnp.concatenate(pieces, axis=1), z).reshape(wacc_ref.shape)

    each(n_j // 4, w_step)

    def wait_ra(t):
        q = chip_peer(n_chip - 1 - t)
        copy(sa1.at[q], ra1.at[q], ssem_ra.at[t], rsem_ra.at[q], at_chip(q)).wait_recv()

    each(n_chip - 1, wait_ra)

    def wait_rb(k):
        @pl.when(jnp.logical_or(k != row, b_col != col))
        def _():
            copy(sb.at[k], rb.at[k], ssem_rb.at[k], rsem_rb.at[k], (k, b_col)).wait_recv()

    each(n_row, wait_rb)

    d_a = jnp.sum(ra1[...].astype(F32), axis=0).astype(BF)
    d_b = jnp.sum(rb[...].astype(F32), axis=0).astype(BF)
    d_both = [
        jnp.concatenate(
            [d_a[r * rank : (r + 1) * rank], d_b[r * rank : (r + 1) * rank]], axis=0
        )
        for r in range(n_res)
    ]
    part_p = jnp.zeros((2 * rank, width), F32)
    for r in range(n_res):
        part_p += dot(d_both[r], normed_ref[r])
    half = width // 2
    part_p = jnp.concatenate([part_p[:, :half], part_p[:, half:]], axis=0)

    w_rows, p_rows = rank * rank // n_col, 4 * rank // n_col

    def fill(i):
        st0[i, :w_rows, :] = (wacc_ref[i] * (1.0 / CHOSEN_SEQUENCES)).astype(BF)

    each(n_col, fill)
    for i in range(n_col):
        st0[i, w_rows : w_rows + p_rows, :] = part_p[i * p_rows : (i + 1) * p_rows].astype(BF)
        st0[i, w_rows + p_rows :, :] = jnp.zeros((st0.shape[1] - w_rows - p_rows, half), BF)
    t_sib = sib_copy(2, st0.at[pl.ds(other * n_chip, n_chip)], rt0)
    t_sib.start()

    def layer_norm_back(r):
        g = lax.dot_general(
            d_both[r], w_both, (((0,), (0,)), ((), ())), preferred_element_type=F32
        )
        g = g * scale_ref[...]
        xhat = xhat_ref[r]
        slope = inv_ref[r] * (
            g
            - jnp.mean(g, axis=-1, keepdims=True)
            - xhat * jnp.mean(g * xhat, axis=-1, keepdims=True)
        )
        slope_ref[r] = slope.astype(BF)

    layer_norm_back(0)
    t_sib.wait_recv()

    def t1_copy(t, q):
        return copy(st1.at[q], rt1.at[chip], ssem_t1.at[t], rsem_t1.at[chip], at_chip(q))

    def send_t1(t):
        q = chip_peer(t + 1)
        st1[q] = (st0[core * n_chip + q].astype(F32) + rt0[q].astype(F32)).astype(BF)
        t1_copy(t, q).start()

    each(n_chip - 1, send_t1)
    rt1[chip] = (st0[core * n_chip + chip].astype(F32) + rt0[chip].astype(F32)).astype(BF)
    layer_norm_back(1)
    layer_norm_back(2)

    def wait_t1(t):
        q = chip_peer(n_chip - 1 - t)
        copy(st1.at[q], rt1.at[q], ssem_t1.at[t], rsem_t1.at[q], at_chip(q)).wait_recv()

    each(n_chip - 1, wait_t1)
    st2[...] = jnp.sum(rt1[...].astype(F32), axis=0).astype(BF)
    rt2[row] = st2[...]

    def t2_copy(t, q):
        return copy(st2, rt2.at[row], ssem_t2.at[t], rsem_t2.at[row], (q, col))

    each(n_row - 1, lambda t: t2_copy(t, row_peer(t + 1)).start())
    layer_norm_back(3)
    layer_norm_back(4)

    def wait_t2(t):
        q = row_peer(n_row - 1 - t)
        copy(st2, rt2.at[q], ssem_t2.at[t], rsem_t2.at[q], (q, col)).wait_recv()

    each(n_row - 1, wait_t2)
    sums_ref[core * n_chip + chip] = jnp.sum(rt2[...].astype(F32), axis=0).astype(BF)

    def t3_copy(t, q):
        block = sums_ref.at[core * n_chip + chip]
        return copy(block, block, ssem_t3.at[t], rsem_t3.at[chip], at_chip(q))

    each(n_chip - 1, lambda t: t3_copy(t, chip_peer(t + 1)).start())
    layer_norm_back(5)

    def wait_t3(t):
        q = chip_peer(n_chip - 1 - t)
        block = sums_ref.at[core * n_chip + q]
        copy(block, block, ssem_t3.at[t], rsem_t3.at[q], at_chip(q)).wait_recv()

    each(n_chip - 1, wait_t3)
    mine = sums_ref.at[pl.ds(core * n_chip, n_chip)]
    theirs = sums_ref.at[pl.ds(other * n_chip, n_chip)]
    sib_copy(4, mine, mine).start()
    sib_copy(4, theirs, theirs).wait_recv()

    def sent_b(k):
        @pl.when(jnp.logical_or(k != row, b_col != col))
        def _():
            b_copy(k).wait_send()

        @pl.when(n_row * col + k != me)
        def _():
            rb_copy(k, source(k)).wait_send()

    each(n_row, sent_b)

    def sent_chip(t):
        q = chip_peer(t + 1)
        for made in (a_copy, ra_copy, t1_copy, t3_copy):
            made(t, q).wait_send()

    each(n_chip - 1, sent_chip)
    each(n_chip, lambda q: a_forward(q).wait_send())
    each(n_row - 1, lambda t: t2_copy(t, row_peer(t + 1)).wait_send())
    ra_sib.wait_send()
    t_sib.wait_send()
    sib_copy(4, mine, mine).wait_send()


def last_kernel(slope_ref, sums_ref, out_ref, grad_a_ref, grad_b_ref, grad_w_ref):
    out_ref[...] = slope_ref[...]
    rank = grad_a_ref.shape[0]
    n = sums_ref.shape[0]
    w_rows, p_rows = rank * rank // n, 4 * rank // n
    pieces = []
    for i in range(n):
        piece = sums_ref[i].astype(F32)
        grad_w_ref[i * w_rows : (i + 1) * w_rows, :] = piece[:w_rows]
        pieces.append(piece[w_rows : w_rows + p_rows])
    both = jnp.concatenate(pieces, axis=0)
    grad_a_ref[...] = jnp.concatenate([both[:rank], both[2 * rank : 3 * rank]], axis=1)
    grad_b_ref[...] = jnp.concatenate([both[rank : 2 * rank], both[3 * rank :]], axis=1)


def shards(
    n_row,
    n_col,
    alignment_embedding,
    chosen_sequence_ids,
    standardizer_scale,
    standardizer_offset,
    first_factor_matrix,
    first_factor_shift,
    second_factor_matrix,
    second_factor_shift,
    final_matrix,
    twosite_delta_cotangent,
):
    width, rank = first_factor_matrix.shape
    n_sel = chosen_sequence_ids.shape[0]
    n_res = alignment_embedding.shape[1]
    n_i, n_j, k_width = twosite_delta_cotangent.shape
    lanes = n_col * SLOT
    chunk = n_res * rank
    w_rows = rank * rank // n_col
    p_rows = 4 * rank // n_col
    n_chip = n_col // 2
    t_rows = -(-(w_rows + p_rows) // 16) * 16
    dma = lambda n: pltpu.SemaphoreType.DMA((n,))
    vmem = pltpu.VMEM
    scratch = [
        vmem((n_res, n_sel, width), F32),
        vmem((n_res, n_sel, 1), F32),
        vmem((n_res, n_sel, width), BF),
        vmem(((n_i + 2) * n_j, k_width), F32),
        vmem((n_j, lanes, k_width), BF),
        vmem((rank, n_j * rank, lanes), BF),
        vmem((rank, n_j * rank, lanes), BF),
        vmem((n_col, chunk, n_sel), BF),
        vmem((chunk, n_sel), BF),
        vmem((n_row, chunk, n_sel), BF),
        vmem((rank * lanes, n_sel), F32),
        vmem((rank * lanes, n_sel), BF),
        vmem((n_sel, n_j * rank), BF),
        vmem((rank * lanes, n_sel), F32),
        vmem((2, n_chip, chunk, n_sel), BF),
        *[vmem((n_chip, chunk, n_sel), BF)] * 3,
        *[vmem((n_row, chunk, n_sel), BF)] * 2,
        vmem((n_col, w_rows, k_width), F32),
        vmem((n_col, t_rows, k_width), BF),
        *[vmem((n_chip, t_rows, k_width), BF)] * 3,
        vmem((t_rows, k_width), BF),
        vmem((n_row, t_rows, k_width), BF),
        *[dma(n) for n in (n_chip, n_chip, n_chip, n_chip, n_row, n_row)],
        *[dma(n) for n in (n_chip, n_chip, n_row, n_row)],
        *[dma(n) for n in (n_chip, n_chip, n_row, n_row, n_chip, n_chip, 6)],
    ]
    whole = pl.BlockSpec(memory_space=pltpu.VMEM)
    shift = jnp.concatenate([first_factor_shift, second_factor_shift]).reshape(2 * rank, 1)
    slope, sums = pl.pallas_call(
        kernel,
        out_shape=(
            jax.ShapeDtypeStruct((n_res, n_sel, width), BF),
            jax.ShapeDtypeStruct((n_col, t_rows, k_width), BF),
        ),
        in_specs=[whole] * 9,
        out_specs=(whole,) * 2,
        scratch_shapes=scratch,
        compiler_params=pltpu.CompilerParams(
            collective_id=0, has_side_effects=True, vmem_limit_bytes=60 * 1024 * 1024
        ),
    )(
        alignment_embedding.transpose(1, 0, 2),
        chosen_sequence_ids.reshape(1, n_sel),
        standardizer_scale.reshape(1, width),
        standardizer_offset.reshape(1, width),
        first_factor_matrix.T,
        second_factor_matrix.T,
        shift,
        final_matrix,
        twosite_delta_cotangent,
    )
    slope, grad_a, grad_b, grad_w = pl.pallas_call(
        last_kernel,
        out_shape=(
            jax.ShapeDtypeStruct((n_res, n_sel, width), BF),
            jax.ShapeDtypeStruct((rank, width), F32),
            jax.ShapeDtypeStruct((rank, width), F32),
            jax.ShapeDtypeStruct((rank * rank, k_width), F32),
        ),
        in_specs=[whole] * 2,
        out_specs=(whole,) * 4,
    )(slope, sums)
    return slope.transpose(1, 0, 2), grad_a.T, grad_b.T, grad_w


def solution(mesh):
    return jax.shard_map(
        functools.partial(shards, mesh.shape["row"], mesh.shape["col"]),
        mesh=mesh,
        in_specs=(
            P(None, ("row", "col"), None),
            P(),
            P(),
            P(),
            P(),
            P(),
            P(),
            P(),
            P(),
            P("row", "col", None),
        ),
        out_specs=(P(None, ("row", "col"), None), P(), P(), P()),
        check_vma=False,
    )
```

time: 83.2 us -> 78.8 us (0.947)
  local copies, waits for them, and re-layouts: 8.48 us -> 0.71 us
  Pallas kernels: 72.9 us -> 76.6 us
    unnamed x4 -> x0, local copies, waits for them, and re-layouts: 6.38 us -> none
    pallas_call x0 -> x1, Pallas kernels: none -> 2.05 us  [shards(): pl.pallas_call(last_kernel, out_shape=(jax.ShapeDtypeStruct((n_res, n_sel...]
    pallas_call x1, Pallas kernels: 72.9 us -> 74.5 us  [shards(): pl.pallas_call(kernel, out_shape=(jax.ShapeDtypeStruct((n_res, n_sel, wid...]
    reshape x1 -> x0, local copies, waits for them, and re-layouts: 1.39 us -> none  [shards(): chosen_sequence_ids.reshape(n_sel, 1)]
where the time goes in v2:
time: 78.8 us; the launch traced here: 78.7 us
  Pallas kernels  76.6 us (97%)
    pallas_call x1, Pallas kernels, shards(): pl.pallas_call(kernel, out_shape=(jax.ShapeDtypeStruct((n_res, n_sel, wid...  74.5 us
    pallas_call x1, Pallas kernels, shards(): pl.pallas_call(last_kernel, out_shape=(jax.ShapeDtypeStruct((n_res, n_sel...  2.05 us

profile of v2, /device:TPU:1, one launch (start us, length us, event | category | flops | bytes accessed | tf_op | source)
XLA Modules:
  0.0 78.7 jit_solution(771677620755617972)
XLA Ops:
  0.6 0.7 maximum_bitcast_fusion
  1.4 0.7 copy.14.shift_ref
  2.1 74.5 %shard_map.129 = (bf16[6,128,256]{2,1,0:T(8,128)(2,1)}, bf16[16,80,128]{2,1,0:T(8,128)(2,1)}) custom-call(bf16[6,512,256]{2,1,0:T(8,128)(2,1)} %bitcast.11, s32[1,128]{1,0:T(1,128)} %bitcast.16, f32[1,256]{1,0:T(1,128)} %bitcast.14, f32[1,256]{1,0:T(1,128)} %bitcast.15, bf16[32,256]{1,0:T(8,128)(2,1)} %bitcast.12, bf16[32,256]{1,0:T(8,128)(2,1)} %bitcast.13, ...), custom_call_target="tpu_custom_call" | custom-call | tf_op jit(solution)/shard_map/pallas_call | solution.py:477
  76.6 2.0 %shard_map.130 = (bf16[6,128,256]{2,1,0:T(8,128)(2,1)}, f32[32,256]{1,0:T(8,128)}, f32[32,256]{1,0:T(8,128)}, f32[1024,128]{1,0:T(8,128)}) custom-call(bf16[6,128,256]{2,1,0:T(8,128)(2,1)} %get-tuple-element.10.slope_ref, bf16[16,80,128]{2,1,0:T(8,128)(2,1)} %get-tuple-element.11.sums_ref), custom_call_target="tpu_custom_call" | custom-call | tf_op jit(solution)/shard_map/pallas_call | solution.py:500

commit v3 on v2

v3 whole, which is shorter than its diff:
```python
import functools

import jax
import jax.numpy as jnp
from jax import lax
from jax.experimental import pallas as pl
from jax.experimental.pallas import tpu as pltpu
from jax.sharding import PartitionSpec as P

CHOSEN_SEQUENCES = 128
SLOT = 8

BF = jnp.bfloat16
F32 = jnp.float32
NN = (((1,), (0,)), ((), ()))
NT = (((1,), (1,)), ((), ()))


def dot(left, right, dims=NN):
    return lax.dot_general(left, right, dims, preferred_element_type=F32)


def kernel(
    emb_hbm, ids_ref, scale_ref, offset_ref, w_a_ref, w_b_ref, shift_ref, final_hbm, dz_hbm,
    slope_ref, sums_ref,
    emb_ref, final_ref, dz_ref, in_sems, xhat_ref, inv_ref, normed_ref, dzf_ref, dzb_ref, d_ref, o_ref,
    abuf, bsend, bbuf, atf_ref, at_ref, bt_ref, daf_ref, sa, ra0, sa1, ra1, sb, rb, d_sum, d_own, wacc_ref,
    st0, rt0, st1, rt1,
    ssem_a, rsem_a, ssem_a2, rsem_a2, ssem_b, rsem_b, ssem_ra, rsem_ra, ssem_rb, rsem_rb,
    t_sems, sib_sems,
):
    n_row, n_col = bbuf.shape[0], abuf.shape[0]
    n_chip = n_col // 2
    n_res, n_sel, width = normed_ref.shape
    rank = w_a_ref.shape[0]
    n_j = n_row * n_res
    lanes = n_col * SLOT
    chunk = n_res * rank
    row, col = lax.axis_index("row"), lax.axis_index("col")
    me = row * n_col + col
    b_col, b_slot = me // n_row, me % n_row
    chip, core = col // 2, col % 2
    other = 1 - core
    sibling = (row, col + 1 - 2 * core)

    def copy(src, dst, send_sem, recv_sem, device):
        return pltpu.make_async_remote_copy(
            src_ref=src, dst_ref=dst, send_sem=send_sem, recv_sem=recv_sem,
            device_id=device, device_id_type=pl.DeviceIdType.MESH,
        )

    def each(count, body):
        lax.fori_loop(0, count, lambda i, _: (body(i), None)[1], None)

    def chip_peer(t):
        return lax.rem(chip + t, n_chip)

    def at_chip(q):
        return (row, 2 * q + core)

    n_ring = n_row * n_chip
    ring = row * n_chip + chip

    def at_ring(u):
        return (u // n_chip, 2 * (u % n_chip) + core)

    def each_ring(body):
        half = n_ring // 2
        each(half, lambda t: body(lax.rem(ring + half + t, n_ring)))
        each(half - 1, lambda t: body(lax.rem(ring + 1 + t, n_ring)))

    def row_peer(t):
        return lax.rem(row + t, n_row)

    owner = ((n_row * col + row) // n_col, (n_row * col + row) % n_col)
    taker = (b_slot, b_col)
    stays = jnp.logical_and(b_slot == row, b_col == col)

    loads = [
        pltpu.make_async_copy(src, dst, in_sems.at[i])
        for i, (src, dst) in enumerate(
            [(emb_hbm, emb_ref), (dz_hbm, dz_ref), (final_hbm, final_ref)]
        )
    ]
    for load in loads:
        load.start()

    barrier = pltpu.get_barrier_semaphore()

    def greet(device):
        pl.semaphore_signal(barrier, inc=1, device_id=device, device_id_type=pl.DeviceIdType.MESH)

    greet(sibling)
    each_ring(lambda u: greet(at_ring(u)))

    @pl.when(jnp.logical_not(stays))
    def _():
        greet(owner)
        greet(taker)

    n_all = emb_ref.shape[1]
    ids = jnp.broadcast_to(ids_ref[...], (n_sel, n_sel)).T
    ids = jnp.concatenate([ids] * (n_all // n_sel), axis=1)
    picks = (lax.broadcasted_iota(jnp.int32, (n_sel, n_all), 1) == ids).astype(F32).astype(BF)
    loads[0].wait()
    w_both = jnp.concatenate([w_a_ref[...], w_b_ref[...]], axis=0)
    for r in range(n_res):
        x = dot(picks, emb_ref[r])
        centred = x - jnp.mean(x, axis=-1, keepdims=True)
        inverse = lax.rsqrt(jnp.mean(centred * centred, axis=-1, keepdims=True) + 1e-05)
        xhat = centred * inverse
        xhat_ref[r] = xhat
        inv_ref[r] = inverse
        normed = (xhat * scale_ref[...] + offset_ref[...]).astype(BF)
        normed_ref[r] = normed
        proj = (dot(w_both, normed, NT) + shift_ref[...]).astype(BF)
        abuf[col, r * rank : (r + 1) * rank, :] = proj[:rank]
        bsend[r * rank : (r + 1) * rank, :] = proj[rank:]

    loads[1].wait()
    loads[2].wait()
    n_i, j_width, k_width = dz_ref.shape
    dzf_ref[pl.ds(0, n_i * j_width), :] = dz_ref[...].astype(F32).reshape(n_i * j_width, k_width)
    dzf_ref[pl.ds(n_i * j_width, 2 * j_width), :] = jnp.zeros((2 * j_width, k_width), F32)
    atf_ref[...] = jnp.zeros(atf_ref.shape, F32)

    def spread(j):
        rows = [
            dzf_ref[pl.ds(n_res * q * j_width + j, SLOT, stride=j_width), :] for q in range(n_col)
        ]
        dzb_ref[j] = jnp.concatenate(rows, axis=0).astype(BF)

    each(n_j, spread)

    pl.semaphore_wait(barrier, n_ring + jnp.where(stays, 0, 2))

    first_b = copy(bsend, bbuf.at[b_slot], sib_sems.at[6], sib_sems.at[7], taker)

    @pl.when(stays)
    def _():
        bbuf[b_slot] = bsend[...]

    @pl.when(jnp.logical_not(stays))
    def _():
        first_b.start()

    def b_copy(t, q):
        return copy(bbuf.at[row], bbuf.at[row], ssem_b.at[t], rsem_b.at[row], (q, col))

    def a_copy(t, q):
        return copy(abuf.at[col], abuf.at[col], ssem_a.at[t], rsem_a.at[chip], at_chip(q))

    def a_forward(q):
        block = abuf.at[2 * q + core]
        return copy(block, block, ssem_a2.at[q], rsem_a2.at[q], sibling)

    each(n_chip - 1, lambda t: a_copy(t, chip_peer(t + 1)).start())
    a_forward(chip).start()

    @pl.when(jnp.logical_not(stays))
    def _():
        copy(bsend, bbuf.at[row], sib_sems.at[6], sib_sems.at[7], owner).wait_recv()

    each(n_row - 1, lambda t: b_copy(t, row_peer(t + 1)).start())

    def d_step(step):
        pair = dzb_ref[pl.ds(2 * step, 2)].reshape(2 * lanes, k_width)
        d = dot(final_ref[...], pair, NT).astype(BF)
        for q in range(2):
            at = pl.ds(pl.multiple_of((2 * step + q) * rank, rank), rank)
            d_ref[:, at, :] = d[:, q * lanes : (q + 1) * lanes].reshape(rank, rank, lanes)

    each(n_j // 2, d_step)

    def wait_b(t):
        q = row_peer(n_row - 1 - t)
        copy(bbuf.at[q], bbuf.at[q], ssem_b.at[t], rsem_b.at[q], (q, col)).wait_recv()

    each(n_row - 1, wait_b)
    right_t = bbuf[...].reshape(n_j * rank, n_sel)
    bt_ref[...] = right_t.T

    def part_a_step(step):
        d = jnp.concatenate([d_ref[2 * step], d_ref[2 * step + 1]], axis=1)
        part = dot(bt_ref[...], d) * (1.0 / CHOSEN_SEQUENCES)
        for q in range(2):
            at = pl.ds(pl.multiple_of((2 * step + q) * lanes, lanes), lanes)
            daf_ref[at, :] = part[:, q * lanes : (q + 1) * lanes].T

    def pass_a(t):
        q = chip_peer(n_chip - 1 - t)
        block = abuf.at[2 * q + core]
        copy(block, block, ssem_a.at[t], rsem_a.at[q], at_chip(q)).wait_recv()
        a_forward(q).start()

    each(n_chip - 1, pass_a)

    each(rank // 8, part_a_step)

    def take_a(q):
        for r in range(n_res):
            atf_ref[pl.ds(q * SLOT + r, rank, stride=lanes), :] = abuf[
                q, r * rank : (r + 1) * rank, :
            ].astype(F32)

    def wait_a(q):
        block = abuf.at[2 * q + other]
        copy(block, block, ssem_a2.at[q], rsem_a2.at[q], sibling).wait_recv()
        take_a(2 * q)
        take_a(2 * q + 1)

    each(n_chip, wait_a)

    def cast_a(c):
        at = pl.ds(pl.multiple_of(c * 4 * lanes, 4 * lanes), 4 * lanes)
        at_ref[at, :] = atf_ref[at, :].astype(BF)

    each(rank // 4, cast_a)

    def rb_copy(t, k):
        return copy(sb.at[k], rb.at[row], ssem_rb.at[t], rsem_rb.at[row], (k, col))

    def part_b_block(k):
        at = pl.ds(pl.multiple_of(k * chunk, chunk), chunk)
        total = jnp.zeros((chunk, n_sel), F32)
        for c in range(0, rank, 2):
            d = jnp.concatenate([d_ref[c, at, :], d_ref[c + 1, at, :]], axis=1)
            total += dot(d, at_ref[c * lanes : (c + 2) * lanes, :])
        return (total * (1.0 / CHOSEN_SEQUENCES)).astype(BF)

    def part_b_step(t):
        k = row_peer(t + 1)
        sb[k] = part_b_block(k)
        rb_copy(t, k).start()

    each(n_row - 1, part_b_step)
    rb[row] = part_b_block(row)

    each(rank // 2 - rank // 8, lambda step: part_a_step(rank // 8 + step))

    def pack_a(q):
        for k in range(2):
            for r in range(n_res):
                sa[k, q, r * rank : (r + 1) * rank, :] = daf_ref[
                    pl.ds((2 * q + k) * SLOT + r, rank, stride=lanes), :
                ].astype(BF)

    each(n_chip, pack_a)

    def sib_copy(i, src, dst):
        return copy(src, dst, sib_sems.at[i], sib_sems.at[i + 1], sibling)

    ra_sib = sib_copy(0, sa.at[other], ra0)
    ra_sib.start()

    def wait_rb(t):
        q = row_peer(n_row - 1 - t)
        copy(sb.at[q], rb.at[q], ssem_rb.at[t], rsem_rb.at[q], (q, col)).wait_recv()

    each(n_row - 1, wait_rb)
    d_sum[...] = jnp.sum(rb[...].astype(F32), axis=0).astype(BF)
    last_b = copy(d_sum, d_own, sib_sems.at[8], sib_sems.at[9], owner)

    @pl.when(stays)
    def _():
        d_own[...] = d_sum[...]

    @pl.when(jnp.logical_not(stays))
    def _():
        last_b.start()

    def o_step(step):
        at = pl.ds(pl.multiple_of(2 * step * lanes, 2 * lanes), 2 * lanes)
        o = dot(bbuf[...].reshape(n_j * rank, n_sel), at_ref[at, :], NT).astype(BF)
        o_ref[2 * step] = o[:, :lanes]
        o_ref[2 * step + 1] = o[:, lanes:]

    each(rank // 8, o_step)

    def ra_copy(t, q):
        return copy(sa1.at[q], ra1.at[chip], ssem_ra.at[t], rsem_ra.at[chip], at_chip(q))

    ra_sib.wait_recv()

    def send_part_a(t):
        q = chip_peer(t + 1)
        sa1[q] = (sa[core, q].astype(F32) + ra0[q].astype(F32)).astype(BF)
        ra_copy(t, q).start()

    each(n_chip - 1, send_part_a)
    ra1[chip] = (sa[core, chip].astype(F32) + ra0[chip].astype(F32)).astype(BF)

    each(rank // 2 - rank // 8, lambda step: o_step(rank // 8 + step))

    w_rows, p_rows = rank * rank // (2 * n_ring), 4 * rank // (2 * n_ring)
    wacc_ref[...] = jnp.zeros(wacc_ref.shape, F32)
    j_group = n_j // 6

    def w_step(step):
        pieces = []
        for q in range(j_group):
            at = pl.ds(pl.multiple_of((j_group * step + q) * rank, rank), rank)
            pieces.append(o_ref[:, at, :].reshape(rank * rank, lanes))
        z = dzb_ref[pl.ds(j_group * step, j_group)].reshape(j_group * lanes, k_width)
        part = dot(jnp.concatenate(pieces, axis=1), z)
        wacc_ref[...] += part.reshape(wacc_ref.shape)

    each(6, w_step)
    def wait_ra(t):
        q = chip_peer(n_chip - 1 - t)
        copy(sa1.at[q], ra1.at[q], ssem_ra.at[t], rsem_ra.at[q], at_chip(q)).wait_recv()

    each(n_chip - 1, wait_ra)

    @pl.when(jnp.logical_not(stays))
    def _():
        copy(d_sum, d_own, sib_sems.at[8], sib_sems.at[9], taker).wait_recv()

    d_a = jnp.sum(ra1[...].astype(F32), axis=0).astype(BF)
    d_b = d_own[...]
    d_both = [
        jnp.concatenate(
            [d_a[r * rank : (r + 1) * rank], d_b[r * rank : (r + 1) * rank]], axis=0
        )
        for r in range(n_res)
    ]
    part_p = jnp.zeros((2 * rank, width), F32)
    for r in range(n_res):
        part_p += dot(d_both[r], normed_ref[r])
    half = width // 2
    part_p = jnp.concatenate([part_p[:, :half], part_p[:, half:]], axis=0)

    st0[:, :w_rows, :] = (wacc_ref[...] * (1.0 / CHOSEN_SEQUENCES)).astype(BF)
    spare = jnp.zeros((2 * n_ring, st0.shape[1] - w_rows - p_rows, half), F32)
    tail = [part_p.reshape(2 * n_ring, p_rows, half), spare]
    st0[:, w_rows:, :] = jnp.concatenate(tail, axis=1).astype(BF)
    t_sib = sib_copy(2, st0.at[pl.ds(other * n_ring, n_ring)], rt0)
    t_sib.start()

    def layer_norm_back(r):
        g = lax.dot_general(
            d_both[r], w_both, (((0,), (0,)), ((), ())), preferred_element_type=F32
        )
        g = g * scale_ref[...]
        xhat = xhat_ref[r]
        slope = inv_ref[r] * (
            g
            - jnp.mean(g, axis=-1, keepdims=True)
            - xhat * jnp.mean(g * xhat, axis=-1, keepdims=True)
        )
        slope_ref[r] = slope.astype(BF)

    layer_norm_back(0)
    t_sib.wait_recv()

    mine = pl.ds(core * n_ring, n_ring)
    others = pl.ds(0, n_ring - 1)
    st1[...] = (st0[mine].astype(F32) + rt0[...].astype(F32)).astype(BF)

    def t1_copy(u, src, dst):
        return copy(src, dst, t_sems.at[0], t_sems.at[1], at_ring(u))

    each_ring(lambda u: t1_copy(u, st1.at[u], rt1.at[ring]).start())
    rt1[ring] = st1[ring]
    for r in range(1, n_res // 2):
        layer_norm_back(r)
    t1_all = t1_copy(ring, st1.at[others], rt1.at[others])
    t1_all.wait_recv()
    sums_ref[core * n_ring + ring] = jnp.sum(rt1[...].astype(F32), axis=0).astype(BF)

    def t2_copy(u, block):
        return copy(block, block, t_sems.at[2], t_sems.at[3], at_ring(u))

    each_ring(lambda u: t2_copy(u, sums_ref.at[core * n_ring + ring]).start())
    for r in range(n_res // 2, n_res):
        layer_norm_back(r)
    t2_all = t2_copy(ring, sums_ref.at[pl.ds(core * n_ring, n_ring - 1)])
    t2_all.wait_recv()
    back = sib_copy(4, sums_ref.at[mine], sums_ref.at[mine])
    theirs = sums_ref.at[pl.ds(other * n_ring, n_ring)]
    back.start()
    sib_copy(4, theirs, theirs).wait_recv()

    @pl.when(jnp.logical_not(stays))
    def _():
        first_b.wait_send()
        last_b.wait_send()

    def sent_row(t):
        q = row_peer(t + 1)
        for made in (b_copy, rb_copy):
            made(t, q).wait_send()

    each(n_row - 1, sent_row)

    def sent_chip(t):
        q = chip_peer(t + 1)
        for made in (a_copy, ra_copy):
            made(t, q).wait_send()

    each(n_chip - 1, sent_chip)
    each(n_chip, lambda q: a_forward(q).wait_send())
    ra_sib.wait_send()
    t_sib.wait_send()

    t1_all.wait_send()
    t2_all.wait_send()
    back.wait_send()


def last_kernel(slope_ref, sums_ref, out_ref, grad_a_ref, grad_b_ref, grad_w_ref):
    out_ref[...] = slope_ref[...]
    rank = grad_a_ref.shape[0]
    n = sums_ref.shape[0]
    w_rows, p_rows = rank * rank // n, 4 * rank // n
    pieces = []
    for i in range(n):
        piece = sums_ref[i].astype(F32)
        grad_w_ref[i * w_rows : (i + 1) * w_rows, :] = piece[:w_rows]
        pieces.append(piece[w_rows : w_rows + p_rows])
    both = jnp.concatenate(pieces, axis=0)
    grad_a_ref[...] = jnp.concatenate([both[:rank], both[2 * rank : 3 * rank]], axis=1)
    grad_b_ref[...] = jnp.concatenate([both[rank : 2 * rank], both[3 * rank :]], axis=1)


def shards(
    n_row,
    n_col,
    alignment_embedding,
    chosen_sequence_ids,
    standardizer_scale,
    standardizer_offset,
    first_factor_matrix,
    first_factor_shift,
    second_factor_matrix,
    second_factor_shift,
    final_matrix,
    twosite_delta_cotangent,
):
    width, rank = first_factor_matrix.shape
    n_sel = chosen_sequence_ids.shape[0]
    n_res = alignment_embedding.shape[1]
    n_i, n_j, k_width = twosite_delta_cotangent.shape
    lanes = n_col * SLOT
    chunk = n_res * rank
    n_ring = n_row * n_col // 2
    w_rows = rank * rank // (2 * n_ring)
    p_rows = 4 * rank // (2 * n_ring)
    n_chip = n_col // 2
    t_rows = -(-(w_rows + p_rows) // 16) * 16
    dma = lambda n: pltpu.SemaphoreType.DMA((n,))
    vmem = pltpu.VMEM
    scratch = [
        vmem((n_res, alignment_embedding.shape[0], width), BF),
        vmem(final_matrix.shape, BF),
        vmem(twosite_delta_cotangent.shape, BF),
        dma(3),
        vmem((n_res, n_sel, width), F32),
        vmem((n_res, n_sel, 1), F32),
        vmem((n_res, n_sel, width), BF),
        vmem(((n_i + 2) * n_j, k_width), F32),
        vmem((n_j, lanes, k_width), BF),
        vmem((rank, n_j * rank, lanes), BF),
        vmem((rank, n_j * rank, lanes), BF),
        vmem((n_col, chunk, n_sel), BF),
        vmem((chunk, n_sel), BF),
        vmem((n_row, chunk, n_sel), BF),
        vmem((rank * lanes, n_sel), F32),
        vmem((rank * lanes, n_sel), BF),
        vmem((n_sel, n_j * rank), BF),
        vmem((rank * lanes, n_sel), F32),
        vmem((2, n_chip, chunk, n_sel), BF),
        *[vmem((n_chip, chunk, n_sel), BF)] * 3,
        *[vmem((n_row, chunk, n_sel), BF)] * 2,
        *[vmem((chunk, n_sel), BF)] * 2,
        vmem((2 * n_ring, w_rows, k_width), F32),
        vmem((2 * n_ring, t_rows, k_width), BF),
        *[vmem((n_ring, t_rows, k_width), BF)] * 3,
        *[dma(n) for n in (n_chip, n_chip, n_chip, n_chip, n_row, n_row)],
        *[dma(n) for n in (n_chip, n_chip, n_row, n_row)],
        dma(4),
        dma(10),
    ]
    whole = pl.BlockSpec(memory_space=pltpu.VMEM)
    hbm = pl.BlockSpec(memory_space=pl.ANY)
    shift = jnp.concatenate([first_factor_shift, second_factor_shift]).reshape(2 * rank, 1)
    slope, sums = pl.pallas_call(
        kernel,
        out_shape=(
            jax.ShapeDtypeStruct((n_res, n_sel, width), BF),
            jax.ShapeDtypeStruct((2 * n_ring, t_rows, k_width), BF),
        ),
        in_specs=[hbm, *[whole] * 6, hbm, hbm],
        out_specs=(whole,) * 2,
        scratch_shapes=scratch,
        compiler_params=pltpu.CompilerParams(
            collective_id=0, has_side_effects=True, vmem_limit_bytes=60 * 1024 * 1024
        ),
    )(
        alignment_embedding.transpose(1, 0, 2),
        chosen_sequence_ids.reshape(1, n_sel),
        standardizer_scale.reshape(1, width),
        standardizer_offset.reshape(1, width),
        first_factor_matrix.T,
        second_factor_matrix.T,
        shift,
        final_matrix,
        twosite_delta_cotangent,
    )
    slope, grad_a, grad_b, grad_w = pl.pallas_call(
        last_kernel,
        out_shape=(
            jax.ShapeDtypeStruct((n_res, n_sel, width), BF),
            jax.ShapeDtypeStruct((rank, width), F32),
            jax.ShapeDtypeStruct((rank, width), F32),
            jax.ShapeDtypeStruct((rank * rank, k_width), F32),
        ),
        in_specs=[whole] * 2,
        out_specs=(whole,) * 4,
    )(slope, sums)
    return slope.transpose(1, 0, 2), grad_a.T, grad_b.T, grad_w


def solution(mesh):
    return jax.shard_map(
        functools.partial(shards, mesh.shape["row"], mesh.shape["col"]),
        mesh=mesh,
        in_specs=(
            P(None, ("row", "col"), None),
            P(),
            P(),
            P(),
            P(),
            P(),
            P(),
            P(),
            P(),
            P("row", "col", None),
        ),
        out_specs=(P(None, ("row", "col"), None), P(), P(), P()),
        check_vma=False,
    )
```

time: 78.8 us -> 73.3 us (0.930)
  Pallas kernels: 76.6 us -> 71 us
    pallas_call x1, Pallas kernels: 74.5 us -> 68.8 us  [shards(): pl.pallas_call(kernel, out_shape=(jax.ShapeDtypeStruct((n_res, n_sel, wid...]
where the time goes in v3:
time: 73.3 us; the launch traced here: 73.1 us
  Pallas kernels  71 us (97%)
  other arithmetic  0.75 us (1%)
    pallas_call x1, Pallas kernels, shards(): pl.pallas_call(kernel, out_shape=(jax.ShapeDtypeStruct((n_res, n_sel, wid...  68.8 us
    pallas_call x1, Pallas kernels, shards(): pl.pallas_call(last_kernel, out_shape=(jax.ShapeDtypeStruct((n_res, n_sel...  2.14 us

profile of v3, /device:TPU:1, one launch (start us, length us, event | category | flops | bytes accessed | tf_op | source)
XLA Modules:
  0.0 73.1 jit_solution(16614782714745596969)
XLA Ops:
  0.6 0.7 %maximum_bitcast_fusion = f32[64,1]{0,1:T(1,128)S(1)} fusion(f32[32]{0:T(128)} %param.17, f32[32]{0:T(128)} %param.15), kind=kLoop, calls=%fused_computation | loop fusion | flops 64 | bytes 512 | tf_op jit(solution)/shard_map/reshape | solution.py:486
  1.4 0.7 copy.14.shift_ref
  2.1 68.8 %shard_map.129 = (bf16[6,128,256]{2,1,0:T(8,128)(2,1)}, bf16[128,16,128]{2,1,0:T(8,128)(2,1)}) custom-call(bf16[6,512,256]{2,1,0:T(8,128)(2,1)} %bitcast.11, s32[1,128]{1,0:T(1,128)} %bitcast.16, f32[1,256]{1,0:T(1,128)} %bitcast.14, f32[1,256]{1,0:T(1,128)} %bitcast.15, bf16[32,256]{1,0:T(8,128)(2,1)} %bitcast.12, bf16[32,256]{1,0:T(8,128)(2,1)} %bitcast.13, ...), custom_call_target="tpu_custom_call" | custom-call | tf_op jit(solution)/shard_map/pallas_call | solution.py:487
  70.9 2.1 %shard_map.130 = (bf16[6,128,256]{2,1,0:T(8,128)(2,1)}, f32[32,256]{1,0:T(8,128)}, f32[32,256]{1,0:T(8,128)}, f32[1024,128]{1,0:T(8,128)}) custom-call(bf16[6,128,256]{2,1,0:T(8,128)(2,1)} %get-tuple-element.10.slope_ref, bf16[128,16,128]{2,1,0:T(8,128)(2,1)} %get-tuple-element.11.sums_ref), custom_call_target="tpu_custom_call" | custom-call | tf_op jit(solution)/shard_map/pallas_call | solution.py:510

commit v4 on v3

--- a/solution.py
+++ b/solution.py
@@ -8,6 +8,7 @@
 from jax.sharding import PartitionSpec as P
 
 CHOSEN_SEQUENCES = 128
+ROWS = 16
 SLOT = 8
 
 BF = jnp.bfloat16
@@ -22,8 +23,8 @@
 
 def kernel(
     emb_hbm, ids_ref, scale_ref, offset_ref, w_a_ref, w_b_ref, shift_ref, final_hbm, dz_hbm,
-    slope_ref, sums_ref,
-    emb_ref, final_ref, dz_ref, in_sems, xhat_ref, inv_ref, normed_ref, dzf_ref, dzb_ref, d_ref, o_ref,
+    slope_hbm, sums_ref,
+    emb_ref, final_ref, dz_ref, slope_ref, in_sems, xhat_ref, inv_ref, normed_ref, dzf_ref, dzb_ref, d_ref, o_ref,
     abuf, bsend, bbuf, atf_ref, at_ref, bt_ref, daf_ref, sa, ra0, sa1, ra1, sb, rb, d_sum, d_own, wacc_ref,
     st0, rt0, st1, rt1,
     ssem_a, rsem_a, ssem_a2, rsem_a2, ssem_b, rsem_b, ssem_ra, rsem_ra, ssem_rb, rsem_rb,
@@ -134,7 +135,7 @@
 
     pl.semaphore_wait(barrier, n_ring + jnp.where(stays, 0, 2))
 
-    first_b = copy(bsend, bbuf.at[b_slot], sib_sems.at[6], sib_sems.at[7], taker)
+    first_b = copy(bsend, bbuf.at[b_slot], sib_sems.at[8], sib_sems.at[9], taker)
 
     @pl.when(stays)
     def _():
@@ -159,7 +160,7 @@
 
     @pl.when(jnp.logical_not(stays))
     def _():
-        copy(bsend, bbuf.at[row], sib_sems.at[6], sib_sems.at[7], owner).wait_recv()
+        copy(bsend, bbuf.at[row], sib_sems.at[8], sib_sems.at[9], owner).wait_recv()
 
     each(n_row - 1, lambda t: b_copy(t, row_peer(t + 1)).start())
 
@@ -259,7 +260,7 @@
 
     each(n_row - 1, wait_rb)
     d_sum[...] = jnp.sum(rb[...].astype(F32), axis=0).astype(BF)
-    last_b = copy(d_sum, d_own, sib_sems.at[8], sib_sems.at[9], owner)
+    last_b = copy(d_sum, d_own, sib_sems.at[10], sib_sems.at[11], owner)
 
     @pl.when(stays)
     def _():
@@ -292,9 +293,8 @@
 
     each(rank // 2 - rank // 8, lambda step: o_step(rank // 8 + step))
 
-    w_rows, p_rows = rank * rank // (2 * n_ring), 4 * rank // (2 * n_ring)
     wacc_ref[...] = jnp.zeros(wacc_ref.shape, F32)
-    j_group = n_j // 6
+    j_group = n_j // 3
 
     def w_step(step):
         pieces = []
@@ -303,9 +303,16 @@
             pieces.append(o_ref[:, at, :].reshape(rank * rank, lanes))
         z = dzb_ref[pl.ds(j_group * step, j_group)].reshape(j_group * lanes, k_width)
         part = dot(jnp.concatenate(pieces, axis=1), z)
-        wacc_ref[...] += part.reshape(wacc_ref.shape)
-
-    each(6, w_step)
+        wacc_ref[...] += part
+
+    each(3, w_step)
+    n_w, n_p = rank * rank // 2 // ROWS, 2 * rank // ROWS
+    n_piece = n_w + n_p
+    w_sum = (wacc_ref[...] * (1.0 / CHOSEN_SEQUENCES)).astype(BF)
+    st0[:, :n_w] = w_sum.reshape(2, n_w, ROWS, k_width)
+    w_sib = sib_copy(2, st0.at[other, pl.ds(0, n_w)], rt0.at[pl.ds(0, n_w)])
+    w_sib.start()
+
     def wait_ra(t):
         q = chip_peer(n_chip - 1 - t)
         copy(sa1.at[q], ra1.at[q], ssem_ra.at[t], rsem_ra.at[q], at_chip(q)).wait_recv()
@@ -314,7 +321,7 @@
 
     @pl.when(jnp.logical_not(stays))
     def _():
-        copy(d_sum, d_own, sib_sems.at[8], sib_sems.at[9], taker).wait_recv()
+        copy(d_sum, d_own, sib_sems.at[10], sib_sems.at[11], taker).wait_recv()
 
     d_a = jnp.sum(ra1[...].astype(F32), axis=0).astype(BF)
     d_b = d_own[...]
@@ -330,12 +337,9 @@
     half = width // 2
     part_p = jnp.concatenate([part_p[:, :half], part_p[:, half:]], axis=0)
 
-    st0[:, :w_rows, :] = (wacc_ref[...] * (1.0 / CHOSEN_SEQUENCES)).astype(BF)
-    spare = jnp.zeros((2 * n_ring, st0.shape[1] - w_rows - p_rows, half), F32)
-    tail = [part_p.reshape(2 * n_ring, p_rows, half), spare]
-    st0[:, w_rows:, :] = jnp.concatenate(tail, axis=1).astype(BF)
-    t_sib = sib_copy(2, st0.at[pl.ds(other * n_ring, n_ring)], rt0)
-    t_sib.start()
+    st0[:, n_w:] = part_p.astype(BF).reshape(2, n_p, ROWS, half)
+    p_sib = sib_copy(6, st0.at[other, pl.ds(n_w, n_p)], rt0.at[pl.ds(n_w, n_p)])
+    p_sib.start()
 
     def layer_norm_back(r):
         g = lax.dot_general(
@@ -351,35 +355,63 @@
         slope_ref[r] = slope.astype(BF)
 
     layer_norm_back(0)
-    t_sib.wait_recv()
-
-    mine = pl.ds(core * n_ring, n_ring)
-    others = pl.ds(0, n_ring - 1)
-    st1[...] = (st0[mine].astype(F32) + rt0[...].astype(F32)).astype(BF)
+    w_sib.wait_recv()
+    p_sib.wait_recv()
+
+    w_every, p_every = n_ring // n_w, n_ring // n_p
+    owns_w = lax.rem(ring, w_every) == 0
+    owns_p = lax.rem(ring, p_every) == 1
+    owns = jnp.logical_or(owns_w, owns_p)
+    piece = jnp.where(owns_w, ring // w_every, n_w + ring // p_every)
+    st1[...] = (st0[core].astype(F32) + rt0[...].astype(F32)).astype(BF)
 
     def t1_copy(u, src, dst):
         return copy(src, dst, t_sems.at[0], t_sems.at[1], at_ring(u))
 
-    each_ring(lambda u: t1_copy(u, st1.at[u], rt1.at[ring]).start())
-    rt1[ring] = st1[ring]
+    def send_piece(i, u):
+        @pl.when(u != ring)
+        def _():
+            t1_copy(u, st1.at[i], rt1.at[ring]).start()
+
+    def send_w(t):
+        i = lax.rem(ring // w_every + n_w // 2 + t, n_w)
+        send_piece(i, w_every * i)
+
+    each(n_w, send_w)
+    each(n_p, lambda i: send_piece(n_w + i, p_every * i + 1))
+
+    @pl.when(owns)
+    def _():
+        rt1[ring] = st1[piece]
+
     for r in range(1, n_res // 2):
         layer_norm_back(r)
-    t1_all = t1_copy(ring, st1.at[others], rt1.at[others])
-    t1_all.wait_recv()
-    sums_ref[core * n_ring + ring] = jnp.sum(rt1[...].astype(F32), axis=0).astype(BF)
-
     def t2_copy(u, block):
         return copy(block, block, t_sems.at[2], t_sems.at[3], at_ring(u))
 
-    each_ring(lambda u: t2_copy(u, sums_ref.at[core * n_ring + ring]).start())
+    @pl.when(owns)
+    def _():
+        arrived = rt1.at[pl.ds(0, n_ring - 1)]
+        t1_copy(ring, arrived, arrived).wait_recv()
+        sums_ref[core, piece] = jnp.sum(rt1[...].astype(F32), axis=0).astype(BF)
+        each_ring(lambda u: t2_copy(u, sums_ref.at[core, piece]).start())
+
     for r in range(n_res // 2, n_res):
         layer_norm_back(r)
-    t2_all = t2_copy(ring, sums_ref.at[pl.ds(core * n_ring, n_ring - 1)])
-    t2_all.wait_recv()
-    back = sib_copy(4, sums_ref.at[mine], sums_ref.at[mine])
-    theirs = sums_ref.at[pl.ds(other * n_ring, n_ring)]
+    slope_out = pltpu.make_async_copy(slope_ref, slope_hbm, in_sems.at[0])
+    slope_out.start()
+
+    @pl.when(owns)
+    def _():
+        t2_copy(ring, sums_ref.at[core, pl.ds(0, n_piece - 1)]).wait_recv()
+
+    @pl.when(jnp.logical_not(owns))
+    def _():
+        t2_copy(ring, sums_ref.at[core, pl.ds(0, n_piece)]).wait_recv()
+
+    back = sib_copy(4, sums_ref.at[core], sums_ref.at[core])
     back.start()
-    sib_copy(4, theirs, theirs).wait_recv()
+    sib_copy(4, sums_ref.at[other], sums_ref.at[other]).wait_recv()
 
     @pl.when(jnp.logical_not(stays))
     def _():
@@ -401,24 +433,31 @@
     each(n_chip - 1, sent_chip)
     each(n_chip, lambda q: a_forward(q).wait_send())
     ra_sib.wait_send()
-    t_sib.wait_send()
-
-    t1_all.wait_send()
-    t2_all.wait_send()
+    w_sib.wait_send()
+    p_sib.wait_send()
+
+    @pl.when(owns)
+    def _():
+        t1_copy(ring, st1.at[pl.ds(0, n_piece - 1)], st1.at[pl.ds(0, n_piece - 1)]).wait_send()
+        sent = rt1.at[pl.ds(0, n_ring - 1)]
+        t2_copy(ring, sent).wait_send()
+
+    @pl.when(jnp.logical_not(owns))
+    def _():
+        t1_copy(ring, st1.at[pl.ds(0, n_piece)], st1.at[pl.ds(0, n_piece)]).wait_send()
+
     back.wait_send()
+    slope_out.wait()
 
 
 def last_kernel(slope_ref, sums_ref, out_ref, grad_a_ref, grad_b_ref, grad_w_ref):
     out_ref[...] = slope_ref[...]
-    rank = grad_a_ref.shape[0]
-    n = sums_ref.shape[0]
-    w_rows, p_rows = rank * rank // n, 4 * rank // n
-    pieces = []
-    for i in range(n):
-        piece = sums_ref[i].astype(F32)
-        grad_w_ref[i * w_rows : (i + 1) * w_rows, :] = piece[:w_rows]
-        pieces.append(piece[w_rows : w_rows + p_rows])
-    both = jnp.concatenate(pieces, axis=0)
+    rank, width = grad_a_ref.shape
+    half = width // 2
+    n_w = rank * rank // 2 // ROWS
+    sums = sums_ref[...].astype(F32)
+    grad_w_ref[...] = sums[:, :n_w].reshape(grad_w_ref.shape)
+    both = sums[:, n_w:].reshape(4 * rank, half)
     grad_a_ref[...] = jnp.concatenate([both[:rank], both[2 * rank : 3 * rank]], axis=1)
     grad_b_ref[...] = jnp.concatenate([both[rank : 2 * rank], both[3 * rank :]], axis=1)
 
@@ -444,16 +483,15 @@
     lanes = n_col * SLOT
     chunk = n_res * rank
     n_ring = n_row * n_col // 2
-    w_rows = rank * rank // (2 * n_ring)
-    p_rows = 4 * rank // (2 * n_ring)
     n_chip = n_col // 2
-    t_rows = -(-(w_rows + p_rows) // 16) * 16
+    n_piece = rank * rank // 2 // ROWS + 2 * rank // ROWS
     dma = lambda n: pltpu.SemaphoreType.DMA((n,))
     vmem = pltpu.VMEM
     scratch = [
         vmem((n_res, alignment_embedding.shape[0], width), BF),
         vmem(final_matrix.shape, BF),
         vmem(twosite_delta_cotangent.shape, BF),
+        vmem((n_res, n_sel, width), BF),
         dma(3),
         vmem((n_res, n_sel, width), F32),
         vmem((n_res, n_sel, 1), F32),
@@ -473,13 +511,14 @@
         *[vmem((n_chip, chunk, n_sel), BF)] * 3,
         *[vmem((n_row, chunk, n_sel), BF)] * 2,
         *[vmem((chunk, n_sel), BF)] * 2,
-        vmem((2 * n_ring, w_rows, k_width), F32),
-        vmem((2 * n_ring, t_rows, k_width), BF),
-        *[vmem((n_ring, t_rows, k_width), BF)] * 3,
+        vmem((rank * rank, k_width), F32),
+        vmem((2, n_piece, ROWS, k_width), BF),
+        *[vmem((n_piece, ROWS, k_width), BF)] * 2,
+        vmem((n_ring, ROWS, k_width), BF),
         *[dma(n) for n in (n_chip, n_chip, n_chip, n_chip, n_row, n_row)],
         *[dma(n) for n in (n_chip, n_chip, n_row, n_row)],
         dma(4),
-        dma(10),
+        dma(12),
     ]
     whole = pl.BlockSpec(memory_space=pltpu.VMEM)
     hbm = pl.BlockSpec(memory_space=pl.ANY)
@@ -488,10 +527,10 @@
         kernel,
         out_shape=(
             jax.ShapeDtypeStruct((n_res, n_sel, width), BF),
-            jax.ShapeDtypeStruct((2 * n_ring, t_rows, k_width), BF),
+            jax.ShapeDtypeStruct((2, n_piece, ROWS, k_width), BF),
         ),
         in_specs=[hbm, *[whole] * 6, hbm, hbm],
-        out_specs=(whole,) * 2,
+        out_specs=(hbm, whole),
         scratch_shapes=scratch,
         compiler_params=pltpu.CompilerParams(
             collective_id=0, has_side_effects=True, vmem_limit_bytes=60 * 1024 * 1024

time: 73.3 us -> 70.8 us (0.966)
  Pallas kernels: 71 us -> 68.4 us
    pallas_call x1, Pallas kernels: 68.8 us -> 66.4 us  [shards(): pl.pallas_call(kernel, out_shape=(jax.ShapeDtypeStruct((n_res, n_sel, wid...]
where the time goes in v4:
time: 70.8 us; the launch traced here: 70.5 us
  Pallas kernels  68.4 us (97%)
  other arithmetic  0.75 us (1%)
  local copies, waits for them, and re-layouts  0.71 us (1%)
    pallas_call x1, Pallas kernels, shards(): pl.pallas_call(kernel, out_shape=(jax.ShapeDtypeStruct((n_res, n_sel, wid...  66.4 us
    pallas_call x1, Pallas kernels, shards(): pl.pallas_call(last_kernel, out_shape=(jax.ShapeDtypeStruct((n_res, n_sel...  2.03 us

profile of v4, /device:TPU:1, one launch (start us, length us, event | category | flops | bytes accessed | tf_op | source)
XLA Modules:
  0.0 70.5 jit_solution(17469576444127742667)
XLA Ops:
  0.6 0.7 %maximum_bitcast_fusion = f32[64,1]{0,1:T(1,128)S(1)} fusion(f32[32]{0:T(128)} %param.17, f32[32]{0:T(128)} %param.15), kind=kLoop, calls=%fused_computation | loop fusion | flops 64 | bytes 512 | tf_op jit(solution)/shard_map/reshape | solution.py:525
  1.4 0.7 %copy.14.shift_ref = f32[64,1]{1,0:T(8,128)} copy(f32[64,1]{0,1:T(1,128)S(1)} %maximum_bitcast_fusion) | data formatting | bytes 512 | tf_op jit(solution)/shard_map/reshape | solution.py:525
  2.1 66.4 %shard_map.129 = (bf16[6,128,256]{2,1,0:T(8,128)(2,1)}, bf16[2,36,16,128]{3,2,1,0:T(8,128)(2,1)}) custom-call(bf16[6,512,256]{2,1,0:T(8,128)(2,1)} %bitcast.11, s32[1,128]{1,0:T(1,128)} %bitcast.16, f32[1,256]{1,0:T(1,128)} %bitcast.14, f32[1,256]{1,0:T(1,128)} %bitcast.15, bf16[32,256]{1,0:T(8,128)(2,1)} %bitcast.12, bf16[32,256]{1,0:T(8,128)(2,1)} %bitcast.13, ...), custom_call_target="tpu_custom_call" | custom-call | tf_op jit(solution)/shard_map/pallas_call | solution.py:526
  68.5 2.0 %shard_map.130 = (bf16[6,128,256]{2,1,0:T(8,128)(2,1)}, f32[32,256]{1,0:T(8,128)}, f32[32,256]{1,0:T(8,128)}, f32[1024,128]{1,0:T(8,128)}) custom-call(bf16[6,128,256]{2,1,0:T(8,128)(2,1)} %get-tuple-element.10.slope_ref, bf16[2,36,16,128]{3,2,1,0:T(8,128)(2,1)} %get-tuple-element.11.sums_ref), custom_call_target="tpu_custom_call" | custom-call | tf_op jit(solution)/shard_map/pallas_call | solution.py:549

commit v5 on v4

--- a/solution.py
+++ b/solution.py
@@ -53,6 +53,16 @@
     def each(count, body):
         lax.fori_loop(0, count, lambda i, _: (body(i), None)[1], None)
 
+    def each_by(size, first, count, body):
+        while count % size:
+            size -= 1
+
+        def several(i):
+            for k in range(size):
+                body(first + size * i + k)
+
+        each(count // size, several)
+
     def chip_peer(t):
         return lax.rem(chip + t, n_chip)
 
@@ -131,7 +141,7 @@
         ]
         dzb_ref[j] = jnp.concatenate(rows, axis=0).astype(BF)
 
-    each(n_j, spread)
+    each_by(4, 0, n_j, spread)
 
     pl.semaphore_wait(barrier, n_ring + jnp.where(stays, 0, 2))
 
@@ -171,7 +181,7 @@
             at = pl.ds(pl.multiple_of((2 * step + q) * rank, rank), rank)
             d_ref[:, at, :] = d[:, q * lanes : (q + 1) * lanes].reshape(rank, rank, lanes)
 
-    each(n_j // 2, d_step)
+    each_by(4, 0, n_j // 2, d_step)
 
     def wait_b(t):
         q = row_peer(n_row - 1 - t)
@@ -196,7 +206,7 @@
 
     each(n_chip - 1, pass_a)
 
-    each(rank // 8, part_a_step)
+    each_by(4, 0, rank // 8, part_a_step)
 
     def take_a(q):
         for r in range(n_res):
@@ -234,10 +244,10 @@
         sb[k] = part_b_block(k)
         rb_copy(t, k).start()
 
-    each(n_row - 1, part_b_step)
+    each_by(n_row - 1, 0, n_row - 1, part_b_step)
     rb[row] = part_b_block(row)
 
-    each(rank // 2 - rank // 8, lambda step: part_a_step(rank // 8 + step))
+    each_by(12, rank // 8, rank // 2 - rank // 8, part_a_step)
 
     def pack_a(q):
         for k in range(2):
@@ -276,7 +286,7 @@
         o_ref[2 * step] = o[:, :lanes]
         o_ref[2 * step + 1] = o[:, lanes:]
 
-    each(rank // 8, o_step)
+    each_by(4, 0, rank // 8, o_step)
 
     def ra_copy(t, q):
         return copy(sa1.at[q], ra1.at[chip], ssem_ra.at[t], rsem_ra.at[chip], at_chip(q))
@@ -291,7 +301,7 @@
     each(n_chip - 1, send_part_a)
     ra1[chip] = (sa[core, chip].astype(F32) + ra0[chip].astype(F32)).astype(BF)
 
-    each(rank // 2 - rank // 8, lambda step: o_step(rank // 8 + step))
+    each_by(12, rank // 8, rank // 2 - rank // 8, o_step)
 
     wacc_ref[...] = jnp.zeros(wacc_ref.shape, F32)
     j_group = n_j // 3

time: 70.8 us -> 67.9 us (0.959)
  Pallas kernels: 68.4 us -> 65.5 us
    pallas_call x1, Pallas kernels: 66.4 us -> 63.5 us  [shards(): pl.pallas_call(kernel, out_shape=(jax.ShapeDtypeStruct((n_res, n_sel, wid...]
where the time goes in v5:
time: 67.9 us; the launch traced here: 67.6 us
  Pallas kernels  65.5 us (96%)
  other arithmetic  0.75 us (1%)
  local copies, waits for them, and re-layouts  0.71 us (1%)
    pallas_call x1, Pallas kernels, shards(): pl.pallas_call(kernel, out_shape=(jax.ShapeDtypeStruct((n_res, n_sel, wid...  63.5 us
    pallas_call x1, Pallas kernels, shards(): pl.pallas_call(last_kernel, out_shape=(jax.ShapeDtypeStruct((n_res, n_sel...  2.03 us

profile of v5, /device:TPU:1, one launch (start us, length us, event | category | flops | bytes accessed | tf_op | source)
XLA Modules:
  0.0 67.6 jit_solution(13630906425883177206)
XLA Ops:
  0.6 0.7 %maximum_bitcast_fusion = f32[64,1]{0,1:T(1,128)S(1)} fusion(f32[32]{0:T(128)} %param.17, f32[32]{0:T(128)} %param.15), kind=kLoop, calls=%fused_computation | loop fusion | flops 64 | bytes 512 | tf_op jit(solution)/shard_map/reshape | solution.py:535
  1.4 0.7 %copy.14.shift_ref = f32[64,1]{1,0:T(8,128)} copy(f32[64,1]{0,1:T(1,128)S(1)} %maximum_bitcast_fusion) | data formatting | bytes 512 | tf_op jit(solution)/shard_map/reshape | solution.py:535
  2.1 63.5 %shard_map.129 = (bf16[6,128,256]{2,1,0:T(8,128)(2,1)}, bf16[2,36,16,128]{3,2,1,0:T(8,128)(2,1)}) custom-call(bf16[6,512,256]{2,1,0:T(8,128)(2,1)} %bitcast.11, s32[1,128]{1,0:T(1,128)} %bitcast.16, f32[1,256]{1,0:T(1,128)} %bitcast.14, f32[1,256]{1,0:T(1,128)} %bitcast.15, bf16[32,256]{1,0:T(8,128)(2,1)} %bitcast.12, bf16[32,256]{1,0:T(8,128)(2,1)} %bitcast.13, ...), custom_call_target="tpu_custom_call" | custom-call | tf_op jit(solution)/shard_map/pallas_call | solution.py:536
  65.6 2.0 %shard_map.130 = (bf16[6,128,256]{2,1,0:T(8,128)(2,1)}, f32[32,256]{1,0:T(8,128)}, f32[32,256]{1,0:T(8,128)}, f32[1024,128]{1,0:T(8,128)}) custom-call(bf16[6,128,256]{2,1,0:T(8,128)(2,1)} %get-tuple-element.10.slope_ref, bf16[2,36,16,128]{3,2,1,0:T(8,128)(2,1)} %get-tuple-element.11.sums_ref), custom_call_target="tpu_custom_call" | custom-call | tf_op jit(solution)/shard_map/pallas_call | solution.py:559

commit v6 on v5

--- a/solution.py
+++ b/solution.py
@@ -264,21 +264,18 @@
     ra_sib = sib_copy(0, sa.at[other], ra0)
     ra_sib.start()
 
-    def wait_rb(t):
-        q = row_peer(n_row - 1 - t)
-        copy(sb.at[q], rb.at[q], ssem_rb.at[t], rsem_rb.at[q], (q, col)).wait_recv()
-
-    each(n_row - 1, wait_rb)
-    d_sum[...] = jnp.sum(rb[...].astype(F32), axis=0).astype(BF)
-    last_b = copy(d_sum, d_own, sib_sems.at[10], sib_sems.at[11], owner)
-
-    @pl.when(stays)
-    def _():
-        d_own[...] = d_sum[...]
-
-    @pl.when(jnp.logical_not(stays))
-    def _():
-        last_b.start()
+    def ra_copy(t, q):
+        return copy(sa1.at[q], ra1.at[chip], ssem_ra.at[t], rsem_ra.at[chip], at_chip(q))
+
+    ra_sib.wait_recv()
+
+    def send_part_a(t):
+        q = chip_peer(t + 1)
+        sa1[q] = (sa[core, q].astype(F32) + ra0[q].astype(F32)).astype(BF)
+        ra_copy(t, q).start()
+
+    each(n_chip - 1, send_part_a)
+    ra1[chip] = (sa[core, chip].astype(F32) + ra0[chip].astype(F32)).astype(BF)
 
     def o_step(step):
         at = pl.ds(pl.multiple_of(2 * step * lanes, 2 * lanes), 2 * lanes)
@@ -288,18 +285,21 @@
 
     each_by(4, 0, rank // 8, o_step)
 
-    def ra_copy(t, q):
-        return copy(sa1.at[q], ra1.at[chip], ssem_ra.at[t], rsem_ra.at[chip], at_chip(q))
-
-    ra_sib.wait_recv()
-
-    def send_part_a(t):
-        q = chip_peer(t + 1)
-        sa1[q] = (sa[core, q].astype(F32) + ra0[q].astype(F32)).astype(BF)
-        ra_copy(t, q).start()
-
-    each(n_chip - 1, send_part_a)
-    ra1[chip] = (sa[core, chip].astype(F32) + ra0[chip].astype(F32)).astype(BF)
+    def wait_rb(t):
+        q = row_peer(n_row - 1 - t)
+        copy(sb.at[q], rb.at[q], ssem_rb.at[t], rsem_rb.at[q], (q, col)).wait_recv()
+
+    each(n_row - 1, wait_rb)
+    d_sum[...] = jnp.sum(rb[...].astype(F32), axis=0).astype(BF)
+    last_b = copy(d_sum, d_own, sib_sems.at[10], sib_sems.at[11], owner)
+
+    @pl.when(stays)
+    def _():
+        d_own[...] = d_sum[...]
+
+    @pl.when(jnp.logical_not(stays))
+    def _():
+        last_b.start()
 
     each_by(12, rank // 8, rank // 2 - rank // 8, o_step)
 

time: 67.9 us -> 66.9 us (0.985)
  Pallas kernels: 65.5 us -> 64.6 us
    pallas_call x1, Pallas kernels: 63.5 us -> 62.5 us  [shards(): pl.pallas_call(kernel, out_shape=(jax.ShapeDtypeStruct((n_res, n_sel, wid...]
where the time goes in v6:
time: 66.9 us; the launch traced here: 66.7 us
  Pallas kernels  64.6 us (97%)
  other arithmetic  0.75 us (1%)
  local copies, waits for them, and re-layouts  0.71 us (1%)
    pallas_call x1, Pallas kernels, shards(): pl.pallas_call(kernel, out_shape=(jax.ShapeDtypeStruct((n_res, n_sel, wid...  62.5 us
    pallas_call x1, Pallas kernels, shards(): pl.pallas_call(last_kernel, out_shape=(jax.ShapeDtypeStruct((n_res, n_sel...  2.03 us

profile of v6, /device:TPU:1, one launch (start us, length us, event | category | flops | bytes accessed | tf_op | source)
XLA Modules:
  0.0 66.7 jit_solution(17918319465026254829)
XLA Ops:
  0.6 0.7 %maximum_bitcast_fusion = f32[64,1]{0,1:T(1,128)S(1)} fusion(f32[32]{0:T(128)} %param.17, f32[32]{0:T(128)} %param.15), kind=kLoop, calls=%fused_computation | loop fusion | flops 64 | bytes 512 | tf_op jit(solution)/shard_map/reshape | solution.py:535
  1.4 0.7 %copy.14.shift_ref = f32[64,1]{1,0:T(8,128)} copy(f32[64,1]{0,1:T(1,128)S(1)} %maximum_bitcast_fusion) | data formatting | bytes 512 | tf_op jit(solution)/shard_map/reshape | solution.py:535
  2.1 62.5 %shard_map.129 = (bf16[6,128,256]{2,1,0:T(8,128)(2,1)}, bf16[2,36,16,128]{3,2,1,0:T(8,128)(2,1)}) custom-call(bf16[6,512,256]{2,1,0:T(8,128)(2,1)} %bitcast.11, s32[1,128]{1,0:T(1,128)} %bitcast.16, f32[1,256]{1,0:T(1,128)} %bitcast.14, f32[1,256]{1,0:T(1,128)} %bitcast.15, bf16[32,256]{1,0:T(8,128)(2,1)} %bitcast.12, bf16[32,256]{1,0:T(8,128)(2,1)} %bitcast.13, ...), custom_call_target="tpu_custom_call" | custom-call | tf_op jit(solution)/shard_map/pallas_call | solution.py:536
  64.6 2.0 %shard_map.130 = (bf16[6,128,256]{2,1,0:T(8,128)(2,1)}, f32[32,256]{1,0:T(8,128)}, f32[32,256]{1,0:T(8,128)}, f32[1024,128]{1,0:T(8,128)}) custom-call(bf16[6,128,256]{2,1,0:T(8,128)(2,1)} %get-tuple-element.10.slope_ref, bf16[2,36,16,128]{3,2,1,0:T(8,128)(2,1)} %get-tuple-element.11.sums_ref), custom_call_target="tpu_custom_call" | custom-call | tf_op jit(solution)/shard_map/pallas_call | solution.py:559
